TPU v7x, 128 devices: a whole 4x4x4 slice. The times are simulated.
128 devices in a mesh: grp: 4 (over y_hi, core), seq: 32 (over y_lo, z, x).
Axes of the slice: x: 4, y: 4 (y_hi: 2, y_lo: 2; y = y_hi * 2 + y_lo), z: 4, core: 2. Of those that a mesh axis runs over, the one named last changes fastest.
Arguments:
- control_x: bfloat16 [10240, 3072], P('seq'), may hold values from -0.29882812 to 0.29882812
- control_qkv: bfloat16 [10240, 3, 1536], P('seq'), may hold values from -40 to 40
- control_out_w: bfloat16 [1536, 3072], replicated, may hold values from -0.15625 to 0.15625
- control_gate: float32 [3072], replicated, may hold values from 1 to 3
- base_x: bfloat16 [10240, 3072], P('seq', 'grp'), may hold values from -0.29882812 to 0.29882812
- base_qkv: bfloat16 [10240, 3, 1536], P('seq', None, 'grp'), may hold values from -40 to 40
- base_out_w: bfloat16 [1536, 3072], P('grp'), may hold values from -0.15625 to 0.15625
- base_gate: float32 [3072], replicated, may hold values from 1 to 3
Outputs:
- control_out: bfloat16 [10240, 3072], P('seq', 'grp')
- base_out: bfloat16 [10240, 3072], P('seq', 'grp')
All inputs are finite; a program needn't handle non-finite values.
Results may differ from a plain program's by a relative error of at most 0.017.
Values may be sent and summed in bfloat16 or wider, within the bound.
A program may use at most 512 MiB of HBM per device.

v0:
```python
import math

import jax
import jax.numpy as jnp
from jax import lax
from jax.sharding import PartitionSpec as P

HD = 128


def online_update(state, queries, pairs):
    best, total, accum = state
    heads = queries.shape[1]
    length = pairs.shape[0]
    keys = pairs[:, 0].reshape(length, heads, HD)
    values = pairs[:, 1].reshape(length, heads, HD)
    scores = jnp.einsum("qhd,khd->hqk", queries, keys, preferred_element_type=jnp.float32) * (
        1.0 / math.sqrt(HD)
    )
    newbest = jnp.maximum(best, jnp.max(scores, axis=2))
    shifted = jnp.exp(scores - newbest[:, :, None])
    total = jnp.sum(shifted, axis=2)
    accum = jnp.einsum(
        "hqk,khd->hqd", shifted.astype(jnp.bfloat16), values, preferred_element_type=jnp.float32
    )
    return (newbest, total, accum)


def start_state(heads, rows):
    return (
        jnp.full((heads, rows), -1e30, jnp.float32),
        jnp.zeros((heads, rows), jnp.float32),
        jnp.zeros((heads, rows, HD), jnp.float32),
    )


def finish(state):
    best, total, accum = state
    heads, rows = total.shape
    result = accum / total[:, :, None]
    return result.transpose(1, 0, 2).reshape(rows, heads * HD).astype(jnp.bfloat16)


def on_device(
    control_x, control_qkv, control_out_w, control_gate, base_x, base_qkv, base_out_w, base_gate
):
    rows = control_x.shape[0]
    width = base_x.shape[1]
    group = lax.axis_index("grp")
    base_cols = base_qkv.shape[2]
    control_part = lax.dynamic_slice_in_dim(control_qkv, group * base_cols, base_cols, 2)
    control_heads = control_part.shape[2] // HD
    base_heads = base_cols // HD
    control_queries = control_part[:, 0].reshape(rows, control_heads, HD)
    base_queries = base_qkv[:, 0].reshape(rows, base_heads, HD)
    initial = (start_state(control_heads, rows), start_state(base_heads, rows))
    control_state = online_update(
        initial[0], control_queries, lax.all_gather(control_part[:, 1:3], "seq", axis=0, tiled=True)
    )
    base_state = online_update(
        initial[1], base_queries, lax.all_gather(base_qkv[:, 1:3], "seq", axis=0, tiled=True)
    )
    control_attention = finish(control_state)
    base_attention = finish(base_state)
    base_term = jnp.dot(base_attention, base_out_w, preferred_element_type=jnp.float32)
    weight_rows = lax.dynamic_slice_in_dim(control_out_w, group * base_cols, base_cols, 0)
    control_term = jnp.dot(control_attention, weight_rows, preferred_element_type=jnp.float32)
    base_proj, control_proj = (
        lax.psum_scatter(
            base_term.astype(jnp.bfloat16), "grp", scatter_dimension=1, tiled=True
        ).astype(jnp.float32),
        lax.psum_scatter(
            control_term.astype(jnp.bfloat16), "grp", scatter_dimension=1, tiled=True
        ).astype(jnp.float32),
    )
    control_cols = lax.dynamic_slice_in_dim(control_x, group * width, width, 1)
    control_gain = lax.dynamic_slice_in_dim(control_gate, group * width, width, 0)
    base_gain = lax.dynamic_slice_in_dim(base_gate, group * width, width, 0)
    control_out = (control_cols.astype(jnp.float32) + control_gain[None, :] * control_proj).astype(
        jnp.bfloat16
    )
    base_out = (
        base_x.astype(jnp.float32)
        + base_gain[None, :] * base_proj
        + control_out.astype(jnp.float32)
    ).astype(jnp.bfloat16)
    return (control_out, base_out)


def solution(mesh):
    in_specs = (
        P("seq", None),
        P("seq", None, None),
        P(),
        P(),
        P("seq", "grp"),
        P("seq", None, "grp"),
        P("grp", None),
        P(),
    )
    out_specs = (P("seq", "grp"), P("seq", "grp"))
    return jax.shard_map(
        on_device, mesh=mesh, in_specs=in_specs, out_specs=out_specs, check_vma=False
    )
```

profile of v0, /device:TPU:1, one launch (start us, length us, event | category | flops | bytes accessed | tf_op | source)
XLA Modules:
  0.0 583.9 jit_solution(6075591299626838709)
XLA Ops:
  7.2 1.2 slice.29
  8.5 1.3 copy.48
  9.9 1.3 copy.45
  11.3 1.0 slice.28
  12.7 174.5 %all-gather.5.cloned.1.call-done = bf16[10240,2,384]{2,1,0:T(2,128)(2,1)} async-done(((bf16[320,2,384]{2,1,0:T(2,128)(2,1)}), bf16[10240,2,384]{2,1,0:T(2,128)(2,1)}) %all-gather.5.cloned.1.call-update) | async-done | bytes 15728656 | tf_op jit(solution)/shard_map/all_gather | solution.py:61
  187.2 31.0 %fusion.35 = (bf16[10240,1,384]{2,1,0:T(2,128)(2,1)}, bf16[10240,1,384]{2,1,0:T(2,128)(2,1)}) fusion(bf16[10240,2,384]{2,1,0:T(2,128)(2,1)} %all-gather.5.cloned.1.call-done), kind=kLoop, calls=%fused_computation.33 | loop fusion | bytes 31457280 | tf_op jit(solution)/shard_map/slice | solution.py:15
  218.2 31.2 %copy.50 = bf16[10240,1,384]{0,2,1:T(8,128)(2,1)} copy(bf16[10240,1,384]{2,1,0:T(2,128)(2,1)} %get-tuple-element.7) | data formatting | bytes 15728640
  249.4 31.1 %copy.49 = bf16[10240,1,384]{0,2,1:T(8,128)(2,1)} copy(bf16[10240,1,384]{2,1,0:T(2,128)(2,1)} %get-tuple-element.6) | data formatting | bytes 15728640
  280.4 17.9 %multiply_reduce_fusion = (f32[3,320]{1,0:T(4,128)S(1)}, f32[3,320,10240]{2,1,0:T(8,128)}) fusion(bf16[320,3,128]{0,2,1:T(8,128)(2,1)S(1)} %bitcast.36, bf16[10240,3,128]{0,2,1:T(8,128)(2,1)} %bitcast.31), kind=kOutput, calls=%fused_computation.2 | convolution fusion | flops 2536242176 | bytes 47435520 | tf_op jit(solution)/shard_map/qhd,khd->hqk/dot_general | solution.py:17
  298.3 17.1 %fusion.2 = f32[3,320]{1,0:T(4,128)S(1)} fusion(f32[3,320,10240]{2,1,0:T(8,128)} %get-tuple-element.9, f32[3,320]{1,0:T(4,128)S(1)} %broadcast_maximum_fusion), kind=kLoop, calls=%fused_computation.6 | loop fusion | flops 29490240 | bytes 39329280 | tf_op jit(solution)/shard_map/reduce_sum | solution.py:22
  315.4 17.9 %fusion.22 = bf16[320,3,128]{2,0,1:T(8,128)(2,1)S(1)} fusion(bf16[10240,3,128]{0,2,1:T(8,128)(2,1)} %bitcast.33, f32[3,320,10240]{2,1,0:T(8,128)} %get-tuple-element.9, f32[3,320]{1,0:T(4,128)S(1)} %broadcast_maximum_fusion, f32[320,3]{0,1:T(4,128)S(1)} %bitcast.39), kind=kOutput, calls=%fused_computation.20 | convolution fusion | flops 2546319360 | bytes 47439360 | tf_op jit(solution)/shard_map/hqk,khd->hqd/dot_general | solution.py:23
  333.6 2.5 convolution_convert_fusion
  336.3 39.5 %all-gather.3.cloned.1.call-done = bf16[10240,2,384]{2,1,0:T(2,128)(2,1)} async-done(((bf16[320,2,384]{2,1,0:T(2,128)(2,1)}), bf16[10240,2,384]{2,1,0:T(2,128)(2,1)}) %all-gather.3.cloned.1.call-update) | async-done | bytes 15728656 | tf_op jit(solution)/shard_map/all_gather | solution.py:58
  375.8 30.8 %fusion.34 = (bf16[10240,1,384]{2,1,0:T(2,128)(2,1)}, bf16[10240,1,384]{2,1,0:T(2,128)(2,1)}) fusion(bf16[10240,2,384]{2,1,0:T(2,128)(2,1)} %all-gather.3.cloned.1.call-done), kind=kLoop, calls=%fused_computation.32 | loop fusion | bytes 31457280 | tf_op jit(solution)/shard_map/slice | solution.py:15
  406.6 31.1 %copy.47 = bf16[10240,1,384]{0,2,1:T(8,128)(2,1)} copy(bf16[10240,1,384]{2,1,0:T(2,128)(2,1)} %get-tuple-element.5) | data formatting | bytes 15728640
  437.7 30.9 %copy.46 = bf16[10240,1,384]{0,2,1:T(8,128)(2,1)} copy(bf16[10240,1,384]{2,1,0:T(2,128)(2,1)} %get-tuple-element.4) | data formatting | bytes 15728640
  468.6 17.5 %multiply_reduce_fusion.1 = (f32[3,320]{1,0:T(4,128)S(1)}, f32[3,320,10240]{2,1,0:T(8,128)}) fusion(bf16[320,3,128]{0,2,1:T(8,128)(2,1)S(1)} %bitcast.35, bf16[10240,3,128]{0,2,1:T(8,128)(2,1)} %bitcast.32), kind=kOutput, calls=%fused_computation.3 | convolution fusion | flops 2536242176 | bytes 47435520 | tf_op jit(solution)/shard_map/qhd,khd->hqk/dot_general | solution.py:17
  486.1 16.8 %fusion = f32[3,320]{1,0:T(4,128)S(1)} fusion(f32[3,320,10240]{2,1,0:T(8,128)} %get-tuple-element.11, f32[3,320]{1,0:T(4,128)S(1)} %broadcast_maximum_fusion.1), kind=kLoop, calls=%fused_computation.4 | loop fusion | flops 29490240 | bytes 39329280 | tf_op jit(solution)/shard_map/reduce_sum | solution.py:22
  503.0 17.5 %fusion.28 = bf16[320,3,128]{2,0,1:T(8,128)(2,1)S(1)} fusion(bf16[10240,3,128]{0,2,1:T(8,128)(2,1)} %bitcast.34, f32[3,320,10240]{2,1,0:T(8,128)} %get-tuple-element.11, f32[3,320]{1,0:T(4,128)S(1)} %broadcast_maximum_fusion.1, f32[320,3]{0,1:T(4,128)S(1)} %bitcast.40), kind=kOutput, calls=%fused_computation.22 | convolution fusion | flops 2546319360 | bytes 47439360 | tf_op jit(solution)/shard_map/hqk,khd->hqd/dot_general | solution.py:23
  520.7 4.2 convolution_convert_fusion.1
  524.9 0.8 dynamic_slice.19
  525.7 0.8 dynamic_slice.16
  526.4 48.1 %reduce-scatter.3.cloned.1.call-done = bf16[320,768]{1,0:T(8,128)(2,1)} async-done(((bf16[320,3072]{1,0:T(8,128)(2,1)}), bf16[320,768]{1,0:T(8,128)(2,1)}) %reduce-scatter.3.cloned.1.call-update) | async-done | bytes 491536 | tf_op jit(solution)/shard_map/reduce_scatter | solution.py:72
  574.6 2.7 add_convert_fusion
  (23 shorter events, 1.4 us)
Async XLA Ops:
  7.2 2.7 copy-start
  7.2 180.0 %all-gather.5.cloned.1.call-start = ((), (), s32[]{:S(2)}) async-start(), calls=%async_computation.4 | async-start | bytes 16220160 | tf_op jit(solution)/shard_map/all_gather | solution.py:61
  9.8 366.0 %all-gather.3.cloned.1.call-start = ((), (), s32[]{:S(2)}) async-start(), calls=%async_computation.2 | async-start | bytes 16220160 | tf_op jit(solution)/shard_map/all_gather | solution.py:58
  11.2 515.2 %reduce-scatter.5.cloned.1.call-start = ((), (), s32[]{:S(2)}) async-start(), calls=%async_computation.5 | async-start | bytes 2457600 | tf_op jit(solution)/shard_map/reduce_scatter | solution.py:69
  315.4 18.2 %copy-start.2 = (bf16[384,3072]{1,0:T(8,128)(2,1)S(1)}, bf16[384,3072]{1,0:T(8,128)(2,1)}, u32[]{:S(2)}) copy-start(bf16[384,3072]{1,0:T(8,128)(2,1)} %param.14) | copy-start | bytes 7077892
  336.1 238.5 %reduce-scatter.3.cloned.1.call-start = ((), (), s32[]{:S(2)}) async-start(), calls=%async_computation.3 | async-start | bytes 2457600 | tf_op jit(solution)/shard_map/reduce_scatter | solution.py:72
  503.0 74.4 %copy-start.1 = (bf16[320,3,1536]{2,0,1:T(8,128)(2,1)S(1)}, bf16[320,3,1536]{2,0,1:T(8,128)(2,1)}, u32[]{:S(2)}) copy-start(bf16[320,3,1536]{2,0,1:T(8,128)(2,1)} %param.9) | copy-start | bytes 8847364
Sparse Core Ops, SparseCore 0:
  10.2 176.9 all-gather.4
  189.4 186.3 all-gather.2
  378.4 49.6 reduce-scatter.4
  525.0 49.5 reduce-scatter.2
where the time goes:
time: 588 us; the launch traced here: 584 us
  waiting for transfers between devices  262 us (45%)
  local copies, waits for them, and re-layouts  193 us (33%)
  matrix products  77.4 us (13%)
  other arithmetic  36.7 us (6%)
  between operations  13.9 us (2%)
    all_gather x1, waiting for transfers between devices, on_device(): lax.all_gather(base_qkv[:, 1:3], 'seq', axis=0, tiled=True)  174 us
    unnamed x12, local copies, waits for them, and re-layouts  127 us
    slice x2, local copies, waits for them, and re-layouts, online_update(): keys = pairs[:, 0].reshape(length, heads, HD)  61.8 us
    reduce_scatter x1, waiting for transfers between devices, on_device(): lax.psum_scatter(control_term.astype(jnp.bfloat16), 'grp', scatter_dimens...  48.1 us
    all_gather x1, waiting for transfers between devices, on_device(): lax.all_gather(control_part[:, 1:3], 'seq', axis=0, tiled=True)  39.5 us
    dot_general x2, matrix products, online_update(): jnp.einsum('hqk,khd->hqd', shifted.astype(jnp.bfloat16), values, preferre...  35.4 us
    dot_general x2, matrix products, online_update(): jnp.einsum('qhd,khd->hqk', queries, keys, preferred_element_type=jnp.floa...  35.3 us
    reduce_sum x2, other arithmetic, online_update(): total = jnp.sum(shifted, axis=2)  33.9 us
  transfers between devices with their start and end apart: 4, of which 3 were waited for; matrix products, arithmetic and copies ran while one was open for 52% of the time, Pallas kernels for 0%

commit v1 on v0

v1 whole, which is shorter than its diff:
```python
import math

import jax
import jax.numpy as jnp
from jax import lax
from jax.experimental import pallas as pl
from jax.experimental.pallas import tpu as pltpu
from jax.sharding import PartitionSpec as P

HD = 128
ROWS = 320
SCALE = 1.4426950408889634 / math.sqrt(HD)
NEG = -1e30
NT = (((1,), (1,)), ((), ()))


def where():
    grp = lax.axis_index("grp")
    seq = lax.axis_index("seq")
    return grp // 2, grp % 2, seq // 16, (seq // 4) % 4, seq % 4


def attend_kernel(
    qkv, control_o, base_o, kv, queries, best, accum, result, q_sem, kv_sem, relay_sem, o_sem, send_sem
):
    half, core, y, z, x = where()
    place = 4 * y + z
    model = x // 2
    here = (half, core, y, z, x)

    def same(a, b):
        hit = a[0] == b[0]
        for left, right in zip(a[1:], b[1:]):
            hit = jnp.logical_and(hit, left == right)
        return hit

    def ident(device):
        return {"grp": 2 * device[0] + device[1], "seq": 16 * device[2] + 4 * device[3] + device[4]}

    barrier = pltpu.get_barrier_semaphore()

    def greet(device):
        pl.semaphore_signal(barrier, inc=1, device_id=ident(device))

    def greet_sources(i, carry):
        greet((half, x % 2, i // 16, (i // 4) % 4, i % 4))
        return carry

    lax.fori_loop(0, 32, greet_sources, 0)

    def greet_control(i, carry):
        chip = (8 * (i % 3) + place) // 3
        greet((i // 6, x // 2, chip // 4, chip % 4, (i // 3) % 2))
        return carry

    lax.fori_loop(0, 12, greet_control, 0)

    def greet_base(i, carry):
        chip = (8 * i + place) // 3
        greet((half, x // 2, chip // 4, chip % 4, 2 + core))
        return carry

    lax.fori_loop(0, 3, greet_base, 0)
    greet((half, 1 - core, y, z, x))
    pl.semaphore_wait(barrier, 33 + jnp.where(model == 0, 24, 6))

    def move(number, source, target, arrived, device, start):
        own = same(device, here)
        remote = pltpu.make_async_remote_copy(
            source, target, send_sem.at[number], arrived, device_id=ident(device)
        )

        @pl.when(jnp.logical_not(own))
        def _():
            if start:
                remote.start()
            else:
                remote.wait_send()

        if start:

            @pl.when(own)
            def _():
                pltpu.make_async_copy(source, target, arrived).start()

    def scatter(start):
        def queries_out(i, carry):
            part, head = i // 3, i % 3
            segment = 8 * head + place
            chip = segment // 3
            move(
                i,
                qkv.at[part, 0, head],
                queries.at[segment % 3, x % 2],
                q_sem.at[0],
                (half, x // 2, chip // 4, chip % 4, 2 * part + core),
                start,
            )
            return carry

        lax.fori_loop(0, 6, queries_out, 0)

        def pairs_out(i, carry):
            part, upper, step = i % 2, (i // 2) % 2, i // 4
            to_y, to_z = (y + upper) % 2, (z + 4 - step) % 4
            chip = 4 * to_y + to_z
            first, last = (3 * chip) // 8, (3 * chip + 2) // 8
            device = (half, y, to_y, to_z, 2 * part + core)
            move(
                6 + i,
                qkv.at[part, pl.ds(1, 2), first],
                kv.at[0, :, z, y, x],
                kv_sem.at[0, z],
                device,
                start,
            )

            @pl.when(last != first)
            def _():
                move(
                    22 + i,
                    qkv.at[part, pl.ds(1, 2), last],
                    kv.at[1, :, z, y, x],
                    kv_sem.at[1, z],
                    device,
                    start,
                )

            return carry

        lax.fori_loop(0, 16, pairs_out, 0)

    scatter(True)

    first, last = (3 * place) // 8, (3 * place + 2) // 8
    for i in range(6):
        best[i] = jnp.full(best.shape[1:], NEG, jnp.float32)
        accum[i] = jnp.zeros(accum.shape[1:], jnp.float32)
    sibling = (half, 1 - core, y, z, x)

    def relay(slot, block):
        return pltpu.make_async_remote_copy(
            kv.at[slot, :, block, core],
            kv.at[slot, :, block, core],
            send_sem.at[38 + 4 * slot + block],
            relay_sem.at[slot, block],
            device_id=ident(sibling),
        )

    def arrive(sem, slot, block, side):
        piece = kv.at[slot, :, block, side]
        pltpu.make_async_copy(piece, piece, sem.at[slot, block]).wait()

    def take_own(block):
        arrive(kv_sem, 0, block, core)
        relay(0, block).start()

        @pl.when(last != first)
        def _():
            arrive(kv_sem, 1, block, core)
            relay(1, block).start()

    def take_sibling(block):
        arrive(relay_sem, 0, block, 1 - core)

        @pl.when(last != first)
        def _():
            arrive(relay_sem, 1, block, 1 - core)

    def update(block, side):
        for i in range(6):
            slot = (3 * place + i // 2) // 8 - first
            keys = kv[slot, 0, block, side].reshape(4 * ROWS, HD)
            values = kv[slot, 1, block, side].reshape(4 * ROWS, HD)
            values = jnp.concatenate([values, jnp.ones_like(values)], axis=1)
            scores = lax.dot_general(
                queries[i // 2, i % 2], keys, NT, preferred_element_type=jnp.float32
            )
            old = best[i][:, :1]
            new = jnp.maximum(old, jnp.max(scores, axis=1, keepdims=True))
            weights = jnp.exp2(scores * SCALE - new * SCALE).astype(jnp.bfloat16)
            keep = jnp.exp2((old - new) * SCALE)
            best[i] = jnp.broadcast_to(new, best.shape[1:])
            accum[i] = accum[i] * keep + jnp.dot(
                weights, values, preferred_element_type=jnp.float32
            )

    whole = queries.at[...]
    pltpu.make_async_copy(whole, whole, q_sem.at[0]).wait()
    take_own(z)

    def step(t, carry):
        block = (z + t) % 4
        update(block, core)

        @pl.when(t < 3)
        def _():
            take_own((block + 1) % 4)

        take_sibling(block)
        update(block, 1 - core)
        return carry

    lax.fori_loop(0, 4, step, 0)

    for i in range(6):
        result[i] = (accum[i][:, :HD] / accum[i][:, HD:]).astype(jnp.bfloat16)

    def home(start):
        for i in range(6):
            segment = 3 * place + i // 2
            head = segment // 8
            token = segment % 8
            owner = (token // 4, token % 4, 2 * core + i % 2)

            @pl.when(model == 0)
            def _():
                column = pl.multiple_of((3 * (2 * half + x) + head) * HD, HD)
                for g in range(4):
                    move(
                        46 + 4 * i + g,
                        result.at[i],
                        control_o.at[:, pl.ds(column, HD)],
                        o_sem.at[0],
                        (g // 2, g % 2) + owner,
                        start,
                    )

            @pl.when(model == 1)
            def _():
                column = pl.multiple_of(head * HD, HD)
                move(
                    70 + i,
                    result.at[i],
                    base_o.at[:, pl.ds(column, HD)],
                    o_sem.at[1],
                    (half, x - 2) + owner,
                    start,
                )

    home(True)
    scatter(False)
    for block in range(4):
        relay(0, block).wait_send()

        @pl.when(last != first)
        def _():
            relay(1, block).wait_send()

    home(False)
    pltpu.make_async_copy(control_o, control_o, o_sem.at[0]).wait()
    pltpu.make_async_copy(base_o, base_o, o_sem.at[1]).wait()


def attend(qkv):
    vmem = pl.BlockSpec(memory_space=pltpu.VMEM)
    return pl.pallas_call(
        attend_kernel,
        out_shape=(
            jax.ShapeDtypeStruct((ROWS, 12 * HD), jnp.bfloat16),
            jax.ShapeDtypeStruct((ROWS, 3 * HD), jnp.bfloat16),
        ),
        in_specs=[vmem],
        out_specs=(vmem, vmem),
        scratch_shapes=[
            pltpu.VMEM((2, 2, 4, 2, 4, ROWS, HD), jnp.bfloat16),
            pltpu.VMEM((3, 2, ROWS, HD), jnp.bfloat16),
            pltpu.VMEM((6, ROWS, HD), jnp.float32),
            pltpu.VMEM((6, ROWS, 2 * HD), jnp.float32),
            pltpu.VMEM((6, ROWS, HD), jnp.bfloat16),
            pltpu.SemaphoreType.DMA((1,)),
            pltpu.SemaphoreType.DMA((2, 4)),
            pltpu.SemaphoreType.DMA((2, 4)),
            pltpu.SemaphoreType.DMA((2,)),
            pltpu.SemaphoreType.DMA((76,)),
        ],
        compiler_params=pltpu.CompilerParams(
            collective_id=0, has_side_effects=True, vmem_limit_bytes=60 * 2**20
        ),
        name="attend",
    )(qkv)


def on_device(
    control_x, control_qkv, control_out_w, control_gate, base_x, base_qkv, base_out_w, base_gate
):
    width = base_x.shape[1]
    group = lax.axis_index("grp")
    columns = base_qkv.shape[2]
    control_part = lax.dynamic_slice_in_dim(control_qkv, group * columns, columns, 2)
    qkv = jnp.stack([control_part, base_qkv]).reshape(2, ROWS, 3, 3, HD).transpose(0, 2, 3, 1, 4)
    control_o, base_o = attend(qkv)
    base_term = jnp.dot(base_o, base_out_w, preferred_element_type=jnp.float32)
    base_proj = lax.psum_scatter(
        base_term.astype(jnp.bfloat16), "grp", scatter_dimension=1, tiled=True
    ).astype(jnp.float32)
    control_w = lax.dynamic_slice_in_dim(control_out_w, group * width, width, 1)
    control_proj = jnp.dot(control_o, control_w, preferred_element_type=jnp.float32)
    control_cols = lax.dynamic_slice_in_dim(control_x, group * width, width, 1)
    control_gain = lax.dynamic_slice_in_dim(control_gate, group * width, width, 0)
    base_gain = lax.dynamic_slice_in_dim(base_gate, group * width, width, 0)
    control_out = (control_cols.astype(jnp.float32) + control_gain[None, :] * control_proj).astype(
        jnp.bfloat16
    )
    base_out = (
        base_x.astype(jnp.float32)
        + base_gain[None, :] * base_proj
        + control_out.astype(jnp.float32)
    ).astype(jnp.bfloat16)
    return (control_out, base_out)


def solution(mesh):
    in_specs = (
        P("seq", None),
        P("seq", None, None),
        P(),
        P(),
        P("seq", "grp"),
        P("seq", None, "grp"),
        P("grp", None),
        P(),
    )
    out_specs = (P("seq", "grp"), P("seq", "grp"))
    return jax.shard_map(
        on_device, mesh=mesh, in_specs=in_specs, out_specs=out_specs, check_vma=False
    )
```

time: 588 us -> 191 us (0.32)
  waiting for transfers between devices: 262 us -> 40.6 us
  local copies, waits for them, and re-layouts: 193 us -> 11.7 us
  Pallas kernels: 0 us -> 114 us
  matrix products: 77.4 us -> 8.46 us
  other arithmetic: 36.7 us -> 2.6 us
    all_gather x2 -> x0, waiting for transfers between devices: 214 us -> none  [the longest x1 174 us: on_device(): lax.all_gather(base_qkv[:, 1:3], 'seq', axis=0, tiled=True)]
    unnamed x12 -> x5, local copies, waits for them, and re-layouts: 127 us -> 2.41 us
    pallas_call x0 -> x1, Pallas kernels: none -> 114 us  [attend(): pl.pallas_call(attend_kernel, out_shape=(jax.ShapeDtypeStruct((ROWS, 12 *...]
    dot_general x6 -> x2, matrix products: 77.4 us -> 8.46 us  [the longest x1 4.34 us: on_device(): base_term = jnp.dot(base_o, base_out_w, preferred_element_type=jnp.float32)]
    slice x8 -> x0, local copies, waits for them, and re-layouts: 64.6 us -> none  [the longest x2 61.8 us: online_update(): keys = pairs[:, 0].reshape(length, heads, HD)]
    reduce_scatter x1 -> x0, waiting for transfers between devices: 48.1 us -> none  [on_device(): lax.psum_scatter(control_term.astype(jnp.bfloat16), 'grp', scatter_dimens...]
    reduce_scatter x1, waiting for transfers between devices: 0.01 us -> 40.6 us  [on_device(): lax.psum_scatter(base_term.astype(jnp.bfloat16), 'grp', scatter_dimension...]
    reduce_sum x2 -> x0, other arithmetic: 33.9 us -> none  [online_update(): total = jnp.sum(shifted, axis=2)]
  transfers between devices with their start and end apart: 4 -> 1, of which waited for: 3 -> 1; matrix products, arithmetic and copies ran while one was open for 52% -> 1% of each run, Pallas kernels for 0% -> 0%
where the time goes in v1:
time: 191 us
  Pallas kernels  114 us (60%)
  waiting for transfers between devices  40.6 us (21%)
  between operations  14.1 us (7%)
  local copies, waits for them, and re-layouts  11.7 us (6%)
  matrix products  8.46 us (4%)
  other arithmetic  2.6 us (1%)
    pallas_call x1, Pallas kernels, attend(): pl.pallas_call(attend_kernel, out_shape=(jax.ShapeDtypeStruct((ROWS, 12 *...  114 us
    reduce_scatter x1, waiting for transfers between devices, on_device(): lax.psum_scatter(base_term.astype(jnp.bfloat16), 'grp', scatter_dimension...  40.6 us
    another operation x2, local copies, waits for them, and re-layouts, on_device(): jnp.stack([control_part, base_qkv]).reshape(2, ROWS, 3, 3, HD)  4.52 us
    dot_general x1, matrix products, on_device(): base_term = jnp.dot(base_o, base_out_w, preferred_element_type=jnp.float32)  4.34 us
    dot_general x1, matrix products, on_device(): jnp.dot(control_o, control_w, preferred_element_type=jnp.float32)  4.13 us
  transfers between devices with their start and end apart: 1, of which 1 were waited for; matrix products, arithmetic and copies ran while one was open for 1% of the time, Pallas kernels for 0%

profile of v1, /device:TPU:1, one launch (start us, length us, event | category | flops | bytes accessed | tf_op | source)
XLA Modules:
  0.0 191.0 jit_solution(11607380767604875712)
XLA Ops:
  7.2 0.0 copy-start
  7.2 0.0 reduce-scatter.2.cloned.1.call-start
  7.2 2.4 %copy.11 = bf16[320,3,384]{0,2,1:T(8,128)(2,1)} copy(bf16[320,3,384]{2,0,1:T(8,128)(2,1)} %param.13) | data formatting | bytes 1474560 | tf_op args[5]
  9.6 2.3 %copy.13 = bf16[1,320,3,3,128]{4,1,3,2,0:T(8,128)(2,1)} copy(bf16[1,320,3,3,128]{1,4,3,2,0:T(8,128)(2,1)} %bitcast.8) | data formatting | bytes 1474560 | tf_op jit(solution)/shard_map/stack | solution.py:291
  11.9 0.0 copy-done
  11.9 0.9 constant_dynamic-slice_fusion
  12.8 2.2 %copy.10 = bf16[320,3,384]{0,2,1:T(8,128)(2,1)} copy(bf16[320,3,384]{2,0,1:T(8,128)(2,1)} %constant_dynamic-slice_fusion) | data formatting | bytes 1474560 | tf_op jit(solution)/shard_map/dynamic_slice | solution.py:290
  15.1 2.3 %copy.12 = bf16[1,320,3,3,128]{4,1,3,2,0:T(8,128)(2,1)} copy(bf16[1,320,3,3,128]{1,4,3,2,0:T(8,128)(2,1)} %bitcast.7) | data formatting | bytes 1474560 | tf_op jit(solution)/shard_map/stack | solution.py:291
  17.3 2.6 %maximum_bitcast_fusion.qkv = bf16[2,3,3,320,128]{4,3,2,1,0:T(8,128)(2,1)} fusion(bf16[1,320,3,3,128]{4,1,3,2,0:T(8,128)(2,1)} %copy.13, bf16[1,320,3,3,128]{4,1,3,2,0:T(8,128)(2,1)} %copy.12), kind=kLoop, calls=%fused_computation.3 | loop fusion | flops 737280 | bytes 2949120 | tf_op jit(solution)/shard_map/transpose | solution.py:291
  19.9 113.6 %attend.1 = (bf16[320,1536]{1,0:T(8,128)(2,1)}, bf16[320,384]{1,0:T(8,128)(2,1)}) custom-call(bf16[2,3,3,320,128]{4,3,2,1,0:T(8,128)(2,1)} %maximum_bitcast_fusion.qkv), custom_call_target="tpu_custom_call" | custom-call | tf_op jit(solution)/shard_map/attend/pallas_call | solution.py:257
  133.6 0.0 copy-start.1
  133.6 4.3 %convolution_convert_fusion = bf16[320,3072]{1,0:T(8,128)(2,1)} fusion(bf16[320,384]{1,0:T(8,128)(2,1)} %get-tuple-element.5, bf16[384,3072]{1,0:T(8,128)(2,1)} %param.14), kind=kOutput, calls=%fused_computation | convolution fusion | flops 755957760 | bytes 4571136 | tf_op jit(solution)/shard_map/dot_general | solution.py:293
  137.9 0.0 reduce-scatter.2.cloned.1.call-update
  138.0 0.8 dynamic_slice.19
  138.7 0.8 dynamic_slice.16
  139.5 40.6 %reduce-scatter.2.cloned.1.call-done = bf16[320,768]{1,0:T(8,128)(2,1)} async-done(((bf16[320,3072]{1,0:T(8,128)(2,1)}), bf16[320,768]{1,0:T(8,128)(2,1)}) %reduce-scatter.2.cloned.1.call-update) | async-done | bytes 491536 | tf_op jit(solution)/shard_map/reduce_scatter | solution.py:294
  180.1 0.0 copy-done.1
  180.1 4.1 %add_convert_fusion = (bf16[320,768]{1,0:T(8,128)(2,1)}, bf16[320,768]{1,0:T(8,128)(2,1)}) fusion(bf16[320,768]{1,0:T(8,128)(2,1)} %reduce-scatter.2.cloned.1.call-done, bf16[320,768]{1,0:T(8,128)(2,1)S(1)} %copy-done.1, f32[768]{0:T(1024)S(1)} %dynamic_slice.19, bf16[320,1536]{1,0:T(8,128)(2,1)} %get-tuple-element.4, bf16[1536,3072]{1,0:T(8,128)(2,1)} %param.10, ...), kind=kOutput, calls=%fused_computation.7 | convolution fusion | flops 757678080 | bytes 5807104 | tf_op jit(solution)/shard_map/dot_general | solution.py:298
Async XLA Ops:
  7.2 4.7 %copy-start = (bf16[320,3,1536]{2,0,1:T(8,128)(2,1)S(1)}, bf16[320,3,1536]{2,0,1:T(8,128)(2,1)}, u32[]{:S(2)}) copy-start(bf16[320,3,1536]{2,0,1:T(8,128)(2,1)} %param.9) | copy-start | bytes 8847364
  7.2 172.9 %reduce-scatter.2.cloned.1.call-start = ((), (), s32[]{:S(2)}) async-start(), calls=%async_computation.1 | async-start | bytes 2457600 | tf_op jit(solution)/shard_map/reduce_scatter | solution.py:294
  133.6 46.5 %copy-start.1 = (bf16[320,768]{1,0:T(8,128)(2,1)S(1)}, bf16[320,768]{1,0:T(8,128)(2,1)}, u32[]{:S(2)}) copy-start(bf16[320,768]{1,0:T(8,128)(2,1)} %param.12) | copy-start | bytes 1474564
Sparse Core Ops, SparseCore 0:
  138.1 41.9 reduce-scatter.1

commit v2 on v0

v2 whole, which is shorter than its diff:
```python
import math

import jax
import jax.numpy as jnp
from jax import lax
from jax.experimental import pallas as pl
from jax.experimental.pallas import tpu as pltpu
from jax.sharding import PartitionSpec as P

HD = 128
ROWS = 320
SCALE = 1.4426950408889634 / math.sqrt(HD)
NEG = -1e30
NT = (((1,), (1,)), ((), ()))


def where():
    grp = lax.axis_index("grp")
    seq = lax.axis_index("seq")
    return grp // 2, grp % 2, seq // 16, (seq // 4) % 4, seq % 4


def attend_kernel(
    control,
    base,
    control_o,
    base_o,
    kv,
    queries,
    best,
    accum,
    part_out,
    part_in,
    result,
    x_sem,
    q_sem,
    z_sem,
    far_sem,
    relay_sem,
    part_sem,
    o_sem,
    send_sem,
):
    half, core, y, z, x = where()
    model = x // 2
    here = (half, core, y, z, x)
    sibling = (half, 1 - core, y, z, x)
    above = (half, core, y, (z + 1) % 4, x)
    below = (half, core, y, (z + 3) % 4, x)
    across = (half, core, 1 - y, z, x)

    def same(a, b):
        hit = a[0] == b[0]
        for left, right in zip(a[1:], b[1:]):
            hit = jnp.logical_and(hit, left == right)
        return hit

    def ident(device):
        return {"grp": 2 * device[0] + device[1], "seq": 16 * device[2] + 4 * device[3] + device[4]}

    barrier = pltpu.get_barrier_semaphore()
    for device in (
        [sibling, above, below, across]
        + [(half, x % 2, y, z, 2 * core + i) for i in range(2)]
        + [(half, x // 2, y, z, 2 + core)]
        + [(i, x // 2, y, z, core) for i in range(2)]
    ):
        pl.semaphore_signal(barrier, inc=1, device_id=ident(device))
    pl.semaphore_wait(barrier, 6 + jnp.where(model == 0, 4, 2))

    sends = []

    def send(source, target, arrived, device, may_be_here=False, when=None):
        remote = pltpu.make_async_remote_copy(
            source, target, send_sem.at[len(sends)], arrived, device_id=ident(device)
        )
        away = None
        if may_be_here:
            own = same(device, here)
            away = jnp.logical_not(own)
            if when is not None:
                own, away = jnp.logical_and(own, when), jnp.logical_and(away, when)

            @pl.when(own)
            def _():
                pltpu.make_async_copy(source, target, arrived).start()

            pl.when(away)(remote.start)
        else:
            away = when
            if when is None:
                remote.start()
            else:
                pl.when(when)(remote.start)
        sends.append((remote, away))

    def finish_sends():
        for remote, away in sends:
            if away is None:
                remote.wait_send()
            else:
                pl.when(away)(remote.wait_send)

    def arrive(ref, sem):
        pltpu.make_async_copy(ref, ref, sem).wait()

    group = 2 * half + core
    columns = pl.ds(pl.multiple_of(group * 3 * HD, 3 * HD), 3 * HD)
    for part, ref in ((0, control.at[:, :, columns]), (1, base)):
        target = (half, x // 2, y, z, 2 * part + core)
        send(ref.at[pl.ds(1, 2)], kv.at[0, 0, x % 2], x_sem.at[x % 2], target, True)
    for part, ref in ((0, control.at[:, :, columns]), (1, base)):
        target = (half, x // 2, y, z, 2 * part + core)
        send(ref.at[0], queries.at[0, x % 2], q_sem.at[0, x % 2], target, True)

    best[...] = jnp.full(best.shape, NEG, jnp.float32)
    accum[...] = jnp.zeros(accum.shape, jnp.float32)

    near = jnp.where(x // 2 == core, x % 2, 1 - x % 2)

    for i in (near, 1 - near):
        arrive(kv.at[0, 0, i], x_sem.at[i])
        send(kv.at[0, 0, i], kv.at[1, 0, i], z_sem.at[0, i], above)
        send(kv.at[0, 0, i], kv.at[2, 0, i], z_sem.at[1, i], below)
        send(kv.at[0, 0, i], kv.at[0, 1, i], relay_sem.at[0, i], sibling)
    for i in (near, 1 - near):
        arrive(queries.at[0, i], q_sem.at[0, i])
        send(queries.at[0, i], queries.at[1, i], q_sem.at[1, i], across)

    def neighbours(i):
        arrive(kv.at[1, 0, i], z_sem.at[0, i])
        send(kv.at[1, 0, i, 0], kv.at[3, 0, i, 0], far_sem.at[0, i], above)
        send(kv.at[1, 0, i], kv.at[1, 1, i], relay_sem.at[1, i], sibling)
        arrive(kv.at[2, 0, i], z_sem.at[1, i])
        send(kv.at[2, 0, i, 1], kv.at[3, 0, i, 1], far_sem.at[1, i], below)
        send(kv.at[2, 0, i], kv.at[2, 1, i], relay_sem.at[2, i], sibling)

    def far(i):
        for j in range(2):
            arrive(kv.at[3, 0, i, j], far_sem.at[j, i])
        send(kv.at[3, 0, i], kv.at[3, 1, i], relay_sem.at[3, i], sibling)

    def relayed(block):
        for i in range(2):
            arrive(kv.at[block, 1, i], relay_sem.at[block, i])

    def update(block, side):
        for head in range(3):
            lanes = pl.ds(head * HD, HD)
            keys = kv[block, :, :, 0, :, lanes].reshape(4 * ROWS, HD)
            values = kv[block, :, :, 1, :, lanes].reshape(4 * ROWS, HD)
            values = jnp.concatenate([values, jnp.ones_like(values)], axis=1)
            for i in range(2):
                scores = lax.dot_general(
                    queries[side, i, :, lanes], keys, NT, preferred_element_type=jnp.float32
                )
                old = best[side, i, head][:, :1]
                new = jnp.maximum(old, jnp.max(scores, axis=1, keepdims=True))
                weights = jnp.exp2(scores * SCALE - new * SCALE).astype(jnp.bfloat16)
                keep = jnp.exp2((old - new) * SCALE)
                best[side, i, head] = jnp.broadcast_to(new, best.shape[3:])
                accum[side, i, head] = accum[side, i, head] * keep + jnp.dot(
                    weights, values, preferred_element_type=jnp.float32
                )

    def both(block):
        def one(side, carry):
            update(block, side)
            return carry

        lax.fori_loop(0, 2, one, 0)

    def outcome(side, i, head):
        total = accum[side, i, head][:, HD:]
        log_sum = best[side, i, head] * SCALE + jnp.log2(total)
        return accum[side, i, head][:, :HD] / total, log_sum

    relayed(0)
    update(0, 0)
    neighbours(0)
    for i in range(2):
        arrive(queries.at[1, i], q_sem.at[1, i])
    update(0, 1)
    neighbours(1)
    relayed(1)
    both(1)
    far(0)
    relayed(2)
    both(2)
    far(1)
    relayed(3)
    update(3, 1)

    lane = lax.broadcasted_iota(jnp.int32, (ROWS, HD), 1)
    for i in range(2):
        packed = jnp.zeros((ROWS, HD), jnp.float32)
        for head in range(3):
            value, rest = outcome(1, i, head)
            part_out[i, :, head * HD : (head + 1) * HD] = value.astype(jnp.bfloat16)
            for j in range(3):
                piece = rest.astype(jnp.bfloat16).astype(jnp.float32)
                packed = jnp.where(lane == 3 * head + j, piece, packed)
                rest = rest - piece
        part_out[i, :, 3 * HD :] = packed.astype(jnp.bfloat16)
        send(part_out.at[i], part_in.at[i], part_sem.at[i], across)
    update(3, 0)

    home_columns = pl.ds(pl.multiple_of((2 * half + x % 2) * 3 * HD, 3 * HD), 3 * HD)
    for i in range(2):
        arrive(part_in.at[i], part_sem.at[i])
        packed = part_in[i, :, 3 * HD :].astype(jnp.float32)
        for head in range(3):
            value, log_sum = outcome(0, i, head)
            other = (
                packed[:, 3 * head : 3 * head + 1]
                + packed[:, 3 * head + 1 : 3 * head + 2]
                + packed[:, 3 * head + 2 : 3 * head + 3]
            )
            top = jnp.maximum(log_sum, other)
            mine = jnp.exp2(log_sum - top)
            theirs = jnp.exp2(other - top)
            theirs_value = part_in[i, :, head * HD : (head + 1) * HD].astype(jnp.float32)
            mixed = (value * mine + theirs_value * theirs) / (mine + theirs)
            result[i, :, head * HD : (head + 1) * HD] = mixed.astype(jnp.bfloat16)
        for g in range(2):
            owner = (g, x % 2, y, z, 2 * core + i)
            target = control_o.at[:, home_columns]
            send(result.at[i], target, o_sem.at[half], owner, True, model == 0)
        owner = (half, x % 2, y, z, 2 * core + i)
        send(result.at[i], base_o, o_sem.at[2], owner, True, model == 1)

    for g in range(2):
        source = control_o.at[:, pl.ds(pl.multiple_of((2 * g + core) * 3 * HD, 3 * HD), 3 * HD)]
        arrive(source, o_sem.at[g])
        send(source, source, o_sem.at[3 + g], sibling)
    for g in range(2):
        target = control_o.at[
            :, pl.ds(pl.multiple_of((2 * g + 1 - core) * 3 * HD, 3 * HD), 3 * HD)
        ]
        arrive(target, o_sem.at[3 + g])
    arrive(base_o, o_sem.at[2])
    finish_sends()


def attend(control, base):
    vmem = pl.BlockSpec(memory_space=pltpu.VMEM)
    anywhere = pl.BlockSpec(memory_space=pl.ANY)
    dma = pltpu.SemaphoreType.DMA
    return pl.pallas_call(
        attend_kernel,
        out_shape=(
            jax.ShapeDtypeStruct((ROWS, 12 * HD), jnp.bfloat16),
            jax.ShapeDtypeStruct((ROWS, 3 * HD), jnp.bfloat16),
        ),
        in_specs=[anywhere, anywhere],
        out_specs=(vmem, vmem),
        scratch_shapes=[
            pltpu.VMEM((4, 2, 2, 2, ROWS, 3 * HD), jnp.bfloat16),
            pltpu.VMEM((2, 2, ROWS, 3 * HD), jnp.bfloat16),
            pltpu.VMEM((2, 2, 3, ROWS, HD), jnp.float32),
            pltpu.VMEM((2, 2, 3, ROWS, 2 * HD), jnp.float32),
            pltpu.VMEM((2, ROWS, 4 * HD), jnp.bfloat16),
            pltpu.VMEM((2, ROWS, 4 * HD), jnp.bfloat16),
            pltpu.VMEM((2, ROWS, 3 * HD), jnp.bfloat16),
            dma((2,)),
            dma((2, 2)),
            dma((2, 2)),
            dma((2, 2)),
            dma((4, 2)),
            dma((2,)),
            dma((5,)),
            dma((40,)),
        ],
        compiler_params=pltpu.CompilerParams(
            collective_id=0, has_side_effects=True, vmem_limit_bytes=60 * 2**20
        ),
        name="attend",
    )(control, base)


def on_device(
    control_x, control_qkv, control_out_w, control_gate, base_x, base_qkv, base_out_w, base_gate
):
    width = base_x.shape[1]
    group = lax.axis_index("grp")
    control_o, base_o = attend(control_qkv.transpose(1, 0, 2), base_qkv.transpose(1, 0, 2))
    base_term = jnp.dot(base_o, base_out_w, preferred_element_type=jnp.float32)
    base_proj = lax.psum_scatter(
        base_term.astype(jnp.bfloat16), "grp", scatter_dimension=1, tiled=True
    ).astype(jnp.float32)
    control_w = lax.dynamic_slice_in_dim(control_out_w, group * width, width, 1)
    control_proj = jnp.dot(control_o, control_w, preferred_element_type=jnp.float32)
    control_cols = lax.dynamic_slice_in_dim(control_x, group * width, width, 1)
    control_gain = lax.dynamic_slice_in_dim(control_gate, group * width, width, 0)
    base_gain = lax.dynamic_slice_in_dim(base_gate, group * width, width, 0)
    control_out = (control_cols.astype(jnp.float32) + control_gain[None, :] * control_proj).astype(
        jnp.bfloat16
    )
    base_out = (
        base_x.astype(jnp.float32)
        + base_gain[None, :] * base_proj
        + control_out.astype(jnp.float32)
    ).astype(jnp.bfloat16)
    return (control_out, base_out)


def solution(mesh):
    in_specs = (
        P("seq", None),
        P("seq", None, None),
        P(),
        P(),
        P("seq", "grp"),
        P("seq", None, "grp"),
        P("grp", None),
        P(),
    )
    out_specs = (P("seq", "grp"), P("seq", "grp"))
    return jax.shard_map(
        on_device, mesh=mesh, in_specs=in_specs, out_specs=out_specs, check_vma=False
    )
```

time: 588 us -> 157 us (0.27)
  waiting for transfers between devices: 262 us -> 39.4 us
  local copies, waits for them, and re-layouts: 193 us -> 1.56 us
  Pallas kernels: 0 us -> 94.6 us
  matrix products: 77.4 us -> 7.48 us
  other arithmetic: 36.7 us -> 0 us
    all_gather x2 -> x0, waiting for transfers between devices: 214 us -> none  [the longest x1 174 us: on_device(): lax.all_gather(base_qkv[:, 1:3], 'seq', axis=0, tiled=True)]
    unnamed x12 -> x4, local copies, waits for them, and re-layouts: 127 us -> 0.01 us
    pallas_call x0 -> x1, Pallas kernels: none -> 94.6 us  [attend(): pl.pallas_call(attend_kernel, out_shape=(jax.ShapeDtypeStruct((ROWS, 12 *...]
    dot_general x6 -> x2, matrix products: 77.4 us -> 7.48 us  [the longest x1 3.98 us: on_device(): jnp.dot(control_o, control_w, preferred_element_type=jnp.float32)]
    slice x8 -> x0, local copies, waits for them, and re-layouts: 64.6 us -> none  [the longest x2 61.8 us: online_update(): keys = pairs[:, 0].reshape(length, heads, HD)]
    reduce_scatter x1 -> x0, waiting for transfers between devices: 48.1 us -> none  [on_device(): lax.psum_scatter(control_term.astype(jnp.bfloat16), 'grp', scatter_dimens...]
    reduce_scatter x1, waiting for transfers between devices: 0.01 us -> 39.4 us  [on_device(): lax.psum_scatter(base_term.astype(jnp.bfloat16), 'grp', scatter_dimension...]
    reduce_sum x2 -> x0, other arithmetic: 33.9 us -> none  [online_update(): total = jnp.sum(shifted, axis=2)]
  transfers between devices with their start and end apart: 4 -> 1, of which waited for: 3 -> 1; matrix products, arithmetic and copies ran while one was open for 52% -> 1% of each run, Pallas kernels for 0% -> 0%
where the time goes in v2:
time: 157 us
  Pallas kernels  94.6 us (60%)
  waiting for transfers between devices  39.4 us (25%)
  between operations  14.1 us (9%)
  matrix products  7.48 us (5%)
    pallas_call x1, Pallas kernels, attend(): pl.pallas_call(attend_kernel, out_shape=(jax.ShapeDtypeStruct((ROWS, 12 *...  94.6 us
    reduce_scatter x1, waiting for transfers between devices, on_device(): lax.psum_scatter(base_term.astype(jnp.bfloat16), 'grp', scatter_dimension...  39.4 us
    dot_general x1, matrix products, on_device(): jnp.dot(control_o, control_w, preferred_element_type=jnp.float32)  3.98 us
    dot_general x1, matrix products, on_device(): base_term = jnp.dot(base_o, base_out_w, preferred_element_type=jnp.float32)  3.51 us
  transfers between devices with their start and end apart: 1, of which 1 were waited for; matrix products, arithmetic and copies ran while one was open for 1% of the time, Pallas kernels for 0%

profile of v2, /device:TPU:1, one launch (start us, length us, event | category | flops | bytes accessed | tf_op | source)
XLA Modules:
  0.0 157.1 jit_solution(8247915562630154128)
XLA Ops:
  7.2 0.0 copy-start
  7.2 0.0 reduce-scatter.2.cloned.1.call-start
  7.2 94.6 %attend.1 = (bf16[320,1536]{1,0:T(8,128)(2,1)}, bf16[320,384]{1,0:T(8,128)(2,1)}) custom-call(bf16[3,320,1536]{2,1,0:T(8,128)(2,1)} %bitcast.5, bf16[3,320,384]{2,1,0:T(8,128)(2,1)} %bitcast.6), custom_call_target="tpu_custom_call" | custom-call | tf_op jit(solution)/shard_map/attend/pallas_call | solution.py:249
  101.8 0.0 copy-done
  101.8 0.0 copy-start.1
  101.8 3.5 %convolution_convert_fusion = bf16[320,3072]{1,0:T(8,128)(2,1)} fusion(bf16[320,384]{1,0:T(8,128)(2,1)} %get-tuple-element.5, bf16[384,3072]{1,0:T(8,128)(2,1)S(1)} %copy-done), kind=kOutput, calls=%fused_computation | convolution fusion | flops 755957760 | bytes 4571136 | tf_op jit(solution)/shard_map/dot_general | solution.py:287
  105.3 0.0 reduce-scatter.2.cloned.1.call-update
  105.4 0.8 dynamic_slice.15
  106.1 0.8 dynamic_slice.13
  106.9 39.4 %reduce-scatter.2.cloned.1.call-done = bf16[320,768]{1,0:T(8,128)(2,1)} async-done(((bf16[320,3072]{1,0:T(8,128)(2,1)}), bf16[320,768]{1,0:T(8,128)(2,1)}) %reduce-scatter.2.cloned.1.call-update) | async-done | bytes 491536 | tf_op jit(solution)/shard_map/reduce_scatter | solution.py:288
  146.3 0.0 copy-done.1
  146.3 4.0 %add_convert_fusion = (bf16[320,768]{1,0:T(8,128)(2,1)}, bf16[320,768]{1,0:T(8,128)(2,1)}) fusion(bf16[320,768]{1,0:T(8,128)(2,1)} %reduce-scatter.2.cloned.1.call-done, bf16[320,768]{1,0:T(8,128)(2,1)} %param.12, f32[768]{0:T(1024)S(1)} %dynamic_slice.15, bf16[320,1536]{1,0:T(8,128)(2,1)S(1)} %copy-done.1, bf16[1536,3072]{1,0:T(8,128)(2,1)} %param.10, ...), kind=kOutput, calls=%fused_computation.6 | convolution fusion | flops 757678080 | bytes 5807104 | tf_op jit(solution)/shard_map/dot_general | solution.py:292
Async XLA Ops:
  7.2 94.6 %copy-start = (bf16[384,3072]{1,0:T(8,128)(2,1)S(1)}, bf16[384,3072]{1,0:T(8,128)(2,1)}, u32[]{:S(2)}) copy-start(bf16[384,3072]{1,0:T(8,128)(2,1)} %param.14) | copy-start | bytes 7077892
  7.2 139.1 %reduce-scatter.2.cloned.1.call-start = ((), (), s32[]{:S(2)}) async-start(), calls=%async_computation.1 | async-start | bytes 2457600 | tf_op jit(solution)/shard_map/reduce_scatter | solution.py:288
  101.8 44.5 %copy-start.1 = (bf16[320,1536]{1,0:T(8,128)(2,1)S(1)}, bf16[320,1536]{1,0:T(8,128)(2,1)}, u32[]{:S(2)}) copy-start(bf16[320,1536]{1,0:T(8,128)(2,1)} %get-tuple-element.4) | copy-start | bytes 2949124
Sparse Core Ops, SparseCore 0:
  105.5 40.7 reduce-scatter.1

commit v3 on v0

v3 whole, which is shorter than its diff:
```python
import math

import jax
import jax.numpy as jnp
from jax import lax
from jax.experimental import pallas as pl
from jax.experimental.pallas import tpu as pltpu
from jax.sharding import PartitionSpec as P

HD = 128
ROWS = 320
WIDTH = 768
GROUP = 3 * HD
SHARE = GROUP // 4
SCALE = 1.4426950408889634 / math.sqrt(HD)
NEG = -1e30
NT = (((1,), (1,)), ((), ()))
PER_HEAD = 31


def sublayer_kernel(
    control_x,
    control,
    control_w,
    control_gate,
    base_x,
    base,
    base_w,
    base_gate,
    control_out,
    base_out,
    kv,
    queries,
    best,
    accum,
    own_value,
    own_sum,
    part_out,
    part_in,
    result,
    merged,
    w_control,
    w_base,
    proj,
    x_control,
    x_base,
    x_sem,
    q_sem,
    z_sem,
    far_sem,
    relay_sem,
    part_sem,
    o_sem,
    hand_sem,
    w_sem,
    local_sem,
    send_sem,
):
    grp = lax.axis_index("grp")
    seq = lax.axis_index("seq")
    half, core, y, z, x = grp // 2, grp % 2, seq // 16, (seq // 4) % 4, seq % 4
    model = x // 2
    here = (half, core, y, z, x)
    sibling = (half, 1 - core, y, z, x)
    above = (half, core, y, (z + 1) % 4, x)
    below = (half, core, y, (z + 3) % 4, x)
    across = (half, core, 1 - y, z, x)

    def ident(device):
        return {"grp": 2 * device[0] + device[1], "seq": 16 * device[2] + 4 * device[3] + device[4]}

    barrier = pltpu.get_barrier_semaphore()
    greeted = (
        [sibling, above, below, across]
        + [(half, x % 2, y, z, 2 * core + i) for i in range(2)]
        + [(f, x // 2, y, z, 2 * m + core) for f in range(2) for m in range(2)]
        + [(1 - half, i, y, z, x) for i in range(2)]
        + [(half, core, y, z, (x + d) % 4) for d in range(1, 4)]
    )
    for device in greeted:
        pl.semaphore_signal(barrier, inc=1, device_id=ident(device))

    lanes_out = pl.ds(pl.multiple_of(grp * WIDTH, WIDTH), WIDTH)
    locals_in = [
        pltpu.make_async_copy(control_w.at[:, :, lanes_out], w_control, local_sem.at[0]),
        pltpu.make_async_copy(base_w.at[:, lanes_out], w_base.at[grp], local_sem.at[1]),
        pltpu.make_async_copy(control_x.at[:, lanes_out], x_control, local_sem.at[2]),
        pltpu.make_async_copy(base_x, x_base, local_sem.at[3]),
    ]

    pl.semaphore_wait(barrier, len(greeted))

    def send(number, source, target, arrived, device, start, may_be_here=False):
        remote = pltpu.make_async_remote_copy(
            source, target, send_sem.at[number], arrived, device_id=ident(device)
        )
        act = remote.start if start else remote.wait_send
        if not may_be_here:
            act()
            return
        own = device[0] == here[0]
        for left, right in zip(device[1:], here[1:]):
            own = jnp.logical_and(own, left == right)
        pl.when(jnp.logical_not(own))(act)
        if start:

            @pl.when(own)
            def _():
                pltpu.make_async_copy(source, target, arrived).start()

    def arrive(ref, sem):
        pltpu.make_async_copy(ref, ref, sem).wait()

    def lanes(index):
        return pl.ds(pl.multiple_of(index * HD, HD), HD)

    def pairs_out(h, start):
        for m, ref, index in ((0, control, 3 * grp + h), (1, base, h)):
            send(
                PER_HEAD * h + m,
                ref.at[pl.ds(1, 2), :, lanes(index)],
                kv.at[h, :, 0, 0, x % 2],
                x_sem.at[h, x % 2],
                (half, x // 2, y, z, 2 * m + core),
                start,
                True,
            )

    def queries_out(h, start):
        for m, ref, index in ((0, control, 3 * grp + h), (1, base, h)):
            send(
                PER_HEAD * h + 2 + m,
                ref.at[0, :, lanes(index)],
                queries.at[h, 0, x % 2],
                q_sem.at[h, 0, x % 2],
                (half, x // 2, y, z, 2 * m + core),
                start,
                True,
            )

    def ring_out(h, i, start):
        block = kv.at[h, :, 0, 0, i]
        number = PER_HEAD * h + i
        send(number + 4, block, kv.at[h, :, 1, 0, i], z_sem.at[h, 0, i], above, start)
        send(number + 6, block, kv.at[h, :, 2, 0, i], z_sem.at[h, 1, i], below, start)
        send(number + 8, block, kv.at[h, :, 0, 1, i], relay_sem.at[h, 0, i], sibling, start)

    def query_across(h, i, start):
        send(
            PER_HEAD * h + 10 + i,
            queries.at[h, 0, i],
            queries.at[h, 1, i],
            q_sem.at[h, 1, i],
            across,
            start,
        )

    def keys_on(h, i, start):
        number = PER_HEAD * h + i
        send(number + 12, kv.at[h, 0, 1, 0, i], kv.at[h, 0, 3, 0, i], far_sem.at[h, 0, i], above, start)
        block = kv.at[h, :, 1, 0, i]
        send(number + 16, block, kv.at[h, :, 1, 1, i], relay_sem.at[h, 1, i], sibling, start)

    def values_on(h, i, start):
        number = PER_HEAD * h + i
        send(number + 14, kv.at[h, 1, 2, 0, i], kv.at[h, 1, 3, 0, i], far_sem.at[h, 1, i], below, start)
        block = kv.at[h, :, 2, 0, i]
        send(number + 18, block, kv.at[h, :, 2, 1, i], relay_sem.at[h, 2, i], sibling, start)

    def far_on(h, i, start):
        block = kv.at[h, :, 3, 0, i]
        send(PER_HEAD * h + 20 + i, block, kv.at[h, :, 3, 1, i], relay_sem.at[h, 3, i], sibling, start)

    def part_across(h, start):
        send(PER_HEAD * h + 22, part_out.at[h], part_in.at[h], part_sem.at[h], across, start)

    def home(h, start):
        for i in range(2):
            for f in range(2):
                send(
                    PER_HEAD * h + 23 + 2 * i + f,
                    result.at[h, i],
                    merged.at[h, model, :, lanes(2 * half + x % 2)],
                    o_sem.at[h, model, half],
                    (f, x % 2, y, z, 2 * core + i),
                    start,
                    True,
                )

    def hand_over(h, m, f, start):
        block = merged.at[h, m, :, lanes(2 * f + core)]
        send(PER_HEAD * h + 27 + 2 * m + f, block, block, hand_sem.at[h, m, f], sibling, start)

    last = 3 * PER_HEAD
    share = pl.ds(pl.multiple_of(SHARE * x, SHARE), SHARE)

    def weights_beside(start):
        columns = pl.ds(pl.multiple_of((2 * half + 1 - core) * WIDTH, WIDTH), WIDTH)
        send(last, base_w.at[:, columns], w_base.at[grp], w_sem.at[0], sibling, start)

    def weights_across(start):
        for c in range(2):
            columns = pl.ds(pl.multiple_of((2 * (1 - half) + c) * WIDTH, WIDTH), WIDTH)
            send(
                last + 1 + c,
                base_w.at[share, columns],
                w_base.at[grp, share],
                w_sem.at[1 + core],
                (1 - half, c, y, z, x),
                start,
            )

    def weights_along(start):
        for d in range(1, 4):
            block = w_base.at[pl.ds(2 * (1 - half), 2), share]
            send(
                last + 2 + d, block, block, w_sem.at[2 + d], (half, core, y, z, (x + d) % 4), start
            )

    near = jnp.where(x // 2 == core, x % 2, 1 - x % 2)

    def blocks_in(h):
        for i in (near, 1 - near):
            arrive(kv.at[h, :, 0, 0, i], x_sem.at[h, i])
            ring_out(h, i, True)
        for i in (near, 1 - near):
            arrive(queries.at[h, 0, i], q_sem.at[h, 0, i])
            query_across(h, i, True)

    def neighbours_in(h):
        for i in (near, 1 - near):
            arrive(kv.at[h, :, 1, 0, i], z_sem.at[h, 0, i])
            keys_on(h, i, True)
            arrive(kv.at[h, :, 2, 0, i], z_sem.at[h, 1, i])
            values_on(h, i, True)

    def far_in(h):
        for i in (near, 1 - near):
            for j in range(2):
                arrive(kv.at[h, j, 3, 0, i], far_sem.at[h, j, i])
            far_on(h, i, True)

    def relayed(h, block):
        for i in range(2):
            arrive(kv.at[h, :, block, 1, i], relay_sem.at[h, block, i])

    def update(h, low, count):
        keys = kv[h, 0, low : low + count].reshape(count * 4 * ROWS, HD)
        values = kv[h, 1, low : low + count].reshape(count * 4 * ROWS, HD)
        values = jnp.concatenate([values, jnp.ones_like(values)], axis=1)
        for side in range(2):
            for i in range(2):
                scores = lax.dot_general(
                    queries[h, side, i], keys, NT, preferred_element_type=jnp.float32
                )
                old = best[side, i][:, :1]
                new = jnp.maximum(old, jnp.max(scores, axis=1, keepdims=True))
                weights = jnp.exp2(scores * SCALE - new * SCALE).astype(jnp.bfloat16)
                keep = jnp.exp2((old - new) * SCALE)
                best[side, i] = jnp.broadcast_to(new, best.shape[2:])
                accum[side, i] = accum[side, i] * keep + jnp.dot(
                    weights, values, preferred_element_type=jnp.float32
                )

    lane = lax.broadcasted_iota(jnp.int32, (ROWS, HD), 1)

    def outcome(side, i):
        total = accum[side, i][:, HD:]
        return accum[side, i][:, :HD] / total, best[side, i] * SCALE + jnp.log2(total)

    def part(h):
        packed = jnp.zeros((ROWS, HD), jnp.float32)
        for i in range(2):
            value, rest = outcome(1, i)
            part_out[h, i] = value.astype(jnp.bfloat16)
            for j in range(3):
                piece = rest.astype(jnp.bfloat16).astype(jnp.float32)
                packed = jnp.where(lane == 3 * i + j, piece, packed)
                rest = rest - piece
        part_out[h, 2] = packed.astype(jnp.bfloat16)
        part_across(h, True)
        for i in range(2):
            own_value[i], own_sum[i] = outcome(0, i)

    def combine(h):
        arrive(part_in.at[h], part_sem.at[h])
        packed = part_in[h, 2].astype(jnp.float32)
        for i in range(2):
            other = (
                packed[:, 3 * i : 3 * i + 1]
                + packed[:, 3 * i + 1 : 3 * i + 2]
                + packed[:, 3 * i + 2 : 3 * i + 3]
            )
            top = jnp.maximum(own_sum[i], other)
            mine = jnp.exp2(own_sum[i] - top)
            theirs = jnp.exp2(other - top)
            mixed = own_value[i] * mine + part_in[h, i].astype(jnp.float32) * theirs
            result[h, i] = (mixed / (mine + theirs)).astype(jnp.bfloat16)
        home(h, True)

    def results_in(h):
        for m in range(2):
            for f in range(2):
                arrive(merged.at[h, m, :, lanes(2 * f + core)], o_sem.at[h, m, f])
                hand_over(h, m, f, True)

    def project(h):
        for m in range(2):
            for f in range(2):
                arrive(merged.at[h, m, :, lanes(2 * f + 1 - core)], hand_sem.at[h, m, f])
        for m, weight in ((0, w_control), (1, w_base)):
            rows = weight[:, h * HD : (h + 1) * HD].reshape(4 * HD, WIDTH)
            term = jnp.dot(merged[h, m], rows, preferred_element_type=jnp.float32)
            proj[m] = term if h == 0 else proj[m] + term

    for h in range(3):
        pairs_out(h, True)
        queries_out(h, True)
    weights_beside(True)
    for copy in locals_in:
        copy.start()
    blocks_in(0)

    def head_step(h, carry):
        best[...] = jnp.full(best.shape, NEG, jnp.float32)
        accum[...] = jnp.zeros(accum.shape, jnp.float32)
        relayed(h, 0)
        for i in range(2):
            arrive(queries.at[h, 1, i], q_sem.at[h, 1, i])
        update(h, 0, 1)

        @pl.when(h < 2)
        def _():
            blocks_in(h + 1)

        neighbours_in(h)

        @pl.when(h == 0)
        def _():
            weights_across(True)

        @pl.when(h == 1)
        def _():
            for c in range(2):
                arrive(w_base.at[2 * (1 - half) + c, share], w_sem.at[1 + c])
            weights_along(True)

        @pl.when(h > 0)
        def _():
            combine(h - 1)

        relayed(h, 1)
        relayed(h, 2)
        update(h, 1, 2)
        far_in(h)
        relayed(h, 3)
        update(h, 3, 1)
        part(h)
        return carry

    lax.fori_loop(0, 3, head_step, 0)

    results_in(0)
    for copy in locals_in:
        copy.wait()
    arrive(w_base.at[2 * half + 1 - core], w_sem.at[0])
    for d in range(1, 4):
        rows = pl.ds(pl.multiple_of(SHARE * ((x + 4 - d) % 4), SHARE), SHARE)
        arrive(w_base.at[pl.ds(2 * (1 - half), 2), rows], w_sem.at[2 + d])
    project(0)
    results_in(1)
    combine(2)
    project(1)
    results_in(2)
    project(2)

    for k in range(WIDTH // HD):
        part_lanes = slice(k * HD, (k + 1) * HD)
        row = pl.ds(grp * (WIDTH // HD) + k, 1)
        first = x_control[:, part_lanes].astype(jnp.float32) + control_gate[row, :] * proj[0, :, part_lanes]
        first = first.astype(jnp.bfloat16)
        control_out[:, part_lanes] = first
        second = x_base[:, part_lanes].astype(jnp.float32) + base_gate[row, :] * proj[1, :, part_lanes]
        base_out[:, part_lanes] = (second + first.astype(jnp.float32)).astype(jnp.bfloat16)

    def finish(h, carry):
        pairs_out(h, False)
        queries_out(h, False)
        for i in range(2):
            ring_out(h, i, False)
            query_across(h, i, False)
            keys_on(h, i, False)
            values_on(h, i, False)
            far_on(h, i, False)
        part_across(h, False)
        home(h, False)
        for m in range(2):
            for f in range(2):
                hand_over(h, m, f, False)
        return carry

    lax.fori_loop(0, 3, finish, 0)
    weights_beside(False)
    weights_across(False)
    weights_along(False)


def on_device(
    control_x, control_qkv, control_out_w, control_gate, base_x, base_qkv, base_out_w, base_gate
):
    vmem = pl.BlockSpec(memory_space=pltpu.VMEM)
    anywhere = pl.BlockSpec(memory_space=pl.ANY)
    dma = pltpu.SemaphoreType.DMA
    half16 = jnp.bfloat16
    full32 = jnp.float32
    shape = jax.ShapeDtypeStruct((ROWS, WIDTH), half16)
    return pl.pallas_call(
        sublayer_kernel,
        out_shape=(shape, shape),
        in_specs=[anywhere, anywhere, anywhere, vmem, anywhere, anywhere, anywhere, vmem],
        out_specs=(vmem, vmem),
        scratch_shapes=[
            pltpu.VMEM((3, 2, 4, 2, 2, ROWS, HD), half16),
            pltpu.VMEM((3, 2, 2, ROWS, HD), half16),
            pltpu.VMEM((2, 2, ROWS, HD), full32),
            pltpu.VMEM((2, 2, ROWS, 2 * HD), full32),
            pltpu.VMEM((2, ROWS, HD), full32),
            pltpu.VMEM((2, ROWS, HD), full32),
            pltpu.VMEM((3, 3, ROWS, HD), half16),
            pltpu.VMEM((3, 3, ROWS, HD), half16),
            pltpu.VMEM((3, 2, ROWS, HD), half16),
            pltpu.VMEM((3, 2, ROWS, 4 * HD), half16),
            pltpu.VMEM((4, GROUP, WIDTH), half16),
            pltpu.VMEM((4, GROUP, WIDTH), half16),
            pltpu.VMEM((2, ROWS, WIDTH), full32),
            pltpu.VMEM((ROWS, WIDTH), half16),
            pltpu.VMEM((ROWS, WIDTH), half16),
            dma((3, 2)),
            dma((3, 2, 2)),
            dma((3, 2, 2)),
            dma((3, 2, 2)),
            dma((3, 4, 2)),
            dma((3,)),
            dma((3, 2, 2)),
            dma((3, 2, 2)),
            dma((6,)),
            dma((4,)),
            dma((3 * PER_HEAD + 6,)),
        ],
        compiler_params=pltpu.CompilerParams(
            collective_id=0, has_side_effects=True, vmem_limit_bytes=60 * 2**20
        ),
        name="sublayer",
    )(
        control_x,
        control_qkv.transpose(1, 0, 2),
        control_out_w.reshape(4, GROUP, 4 * WIDTH),
        control_gate.reshape(4 * WIDTH // HD, HD),
        base_x,
        base_qkv.transpose(1, 0, 2),
        base_out_w,
        base_gate.reshape(4 * WIDTH // HD, HD),
    )


def solution(mesh):
    in_specs = (
        P("seq", None),
        P("seq", None, None),
        P(),
        P(),
        P("seq", "grp"),
        P("seq", None, "grp"),
        P("grp", None),
        P(),
    )
    out_specs = (P("seq", "grp"), P("seq", "grp"))
    return jax.shard_map(
        on_device, mesh=mesh, in_specs=in_specs, out_specs=out_specs, check_vma=False
    )
```

time: 588 us -> 101 us (0.17)
  waiting for transfers between devices: 262 us -> 0 us
  local copies, waits for them, and re-layouts: 193 us -> 3.68 us
  Pallas kernels: 0 us -> 96.3 us
  matrix products: 77.4 us -> 0 us
  other arithmetic: 36.7 us -> 0 us
  between operations: 13.9 us -> 0.64 us
    all_gather x2 -> x0, waiting for transfers between devices: 214 us -> none  [the longest x1 174 us: on_device(): lax.all_gather(base_qkv[:, 1:3], 'seq', axis=0, tiled=True)]
    unnamed x12 -> x2, local copies, waits for them, and re-layouts: 127 us -> 3.68 us
    pallas_call x0 -> x1, Pallas kernels: none -> 96.3 us  [on_device(): pl.pallas_call(sublayer_kernel, out_shape=(shape, shape), in_specs=[anywh...]
    dot_general x6 -> x0, matrix products: 77.4 us -> none  [the longest x2 35.4 us: online_update(): jnp.einsum('hqk,khd->hqd', shifted.astype(jnp.bfloat16), values, preferre...]
    slice x8 -> x0, local copies, waits for them, and re-layouts: 64.6 us -> none  [the longest x2 61.8 us: online_update(): keys = pairs[:, 0].reshape(length, heads, HD)]
    reduce_scatter x2 -> x0, waiting for transfers between devices: 48.1 us -> none  [the longest x1 48.1 us: on_device(): lax.psum_scatter(control_term.astype(jnp.bfloat16), 'grp', scatter_dimens...]
    reduce_sum x2 -> x0, other arithmetic: 33.9 us -> none  [online_update(): total = jnp.sum(shifted, axis=2)]
  transfers between devices with their start and end apart: 4 -> 0, of which waited for: 3 -> 0; matrix products, arithmetic and copies ran while one was open for 52% -> 0% of each run, Pallas kernels for 0% -> 0%
where the time goes in v3:
time: 101 us
  Pallas kernels  96.3 us (95%)
  local copies, waits for them, and re-layouts  3.68 us (4%)
    pallas_call x1, Pallas kernels, on_device(): pl.pallas_call(sublayer_kernel, out_shape=(shape, shape), in_specs=[anywh...  96.3 us
    unnamed x2, local copies, waits for them, and re-layouts  3.68 us

profile of v3, /device:TPU:1, one launch (start us, length us, event | category | flops | bytes accessed | tf_op | source)
XLA Modules:
  0.0 100.6 jit_solution(7772629690539582574)
XLA Ops:
  0.6 96.3 %sublayer.1 = (bf16[320,768]{1,0:T(8,128)(2,1)}, bf16[320,768]{1,0:T(8,128)(2,1)}) custom-call(bf16[320,3072]{1,0:T(8,128)(2,1)} %control_x.1, bf16[3,320,1536]{2,1,0:T(8,128)(2,1)} %bitcast.6, bf16[4,384,3072]{2,1,0:T(8,128)(2,1)} %bitcast.5, f32[24,128]{1,0:T(8,128)} %bitcast.8, bf16[320,768]{1,0:T(8,128)(2,1)} %base_x.1, bf16[3,320,384]{2,1,0:T(8,128)(2,1)} %bitcast.7, ...), custom_call_target="tpu_custom_call" | custom-call | tf_op jit(solution)/shard_map/sublayer/pallas_call | solution.py:417
  97.0 1.8 %copy.12 = bf16[320,768]{1,0:T(8,128)(2,1)} copy(bf16[320,768]{1,0:T(8,128)(2,1)} %get-tuple-element.4) | data formatting | bytes 983040
  98.8 1.8 %copy.13 = bf16[320,768]{1,0:T(8,128)(2,1)} copy(bf16[320,768]{1,0:T(8,128)(2,1)} %get-tuple-element.5) | data formatting | bytes 983040

commit v4 on v3

--- a/solution.py
+++ b/solution.py
@@ -33,8 +33,6 @@
     queries,
     best,
     accum,
-    own_value,
-    own_sum,
     part_out,
     part_in,
     result,
@@ -72,8 +70,8 @@
     barrier = pltpu.get_barrier_semaphore()
     greeted = (
         [sibling, above, below, across]
-        + [(half, x % 2, y, z, 2 * core + i) for i in range(2)]
-        + [(f, x // 2, y, z, 2 * m + core) for f in range(2) for m in range(2)]
+        + [(half, x % 2, p, z, 2 * core + i) for i in range(2) for p in (y, 1 - y)]
+        + [(f, x // 2, p, z, 2 * m + core) for f in range(2) for m in range(2) for p in (y, 1 - y)]
         + [(1 - half, i, y, z, x) for i in range(2)]
         + [(half, core, y, z, (x + d) % 4) for d in range(1, 4)]
     )
@@ -114,26 +112,34 @@
     def lanes(index):
         return pl.ds(pl.multiple_of(index * HD, HD), HD)
 
-    def pairs_out(h, start):
-        for m, ref, index in ((0, control, 3 * grp + h), (1, base, h)):
+    def route(slot):
+        if slot == 1:
+            return 1, y
+        plane = y if slot == 0 else 1 - y
+        return 2 * plane, plane
+
+    def pairs_out(slot, start):
+        head, plane = route(slot)
+        for m, ref, index in ((0, control, 3 * grp + head), (1, base, head)):
             send(
-                PER_HEAD * h + m,
+                PER_HEAD * slot + m,
                 ref.at[pl.ds(1, 2), :, lanes(index)],
-                kv.at[h, :, 0, 0, x % 2],
-                x_sem.at[h, x % 2],
-                (half, x // 2, y, z, 2 * m + core),
+                kv.at[slot, :, 0, 0, x % 2],
+                x_sem.at[slot, x % 2],
+                (half, x // 2, plane, z, 2 * m + core),
                 start,
                 True,
             )
 
-    def queries_out(h, start):
-        for m, ref, index in ((0, control, 3 * grp + h), (1, base, h)):
+    def queries_out(slot, start):
+        head, plane = route(slot)
+        for m, ref, index in ((0, control, 3 * grp + head), (1, base, head)):
             send(
-                PER_HEAD * h + 2 + m,
+                PER_HEAD * slot + 2 + m,
                 ref.at[0, :, lanes(index)],
-                queries.at[h, 0, x % 2],
-                q_sem.at[h, 0, x % 2],
-                (half, x // 2, y, z, 2 * m + core),
+                queries.at[slot % 2, slot // 2, x % 2],
+                q_sem.at[slot % 2, slot // 2, x % 2],
+                (half, x // 2, plane, z, 2 * m + core),
                 start,
                 True,
             )
@@ -145,12 +151,12 @@
         send(number + 6, block, kv.at[h, :, 2, 0, i], z_sem.at[h, 1, i], below, start)
         send(number + 8, block, kv.at[h, :, 0, 1, i], relay_sem.at[h, 0, i], sibling, start)
 
-    def query_across(h, i, start):
+    def query_across(i, start):
         send(
-            PER_HEAD * h + 10 + i,
-            queries.at[h, 0, i],
-            queries.at[h, 1, i],
-            q_sem.at[h, 1, i],
+            PER_HEAD + 10 + i,
+            queries.at[1, 0, i],
+            queries.at[1, 1, i],
+            q_sem.at[1, 1, i],
             across,
             start,
         )
@@ -171,18 +177,19 @@
         block = kv.at[h, :, 3, 0, i]
         send(PER_HEAD * h + 20 + i, block, kv.at[h, :, 3, 1, i], relay_sem.at[h, 3, i], sibling, start)
 
-    def part_across(h, start):
-        send(PER_HEAD * h + 22, part_out.at[h], part_in.at[h], part_sem.at[h], across, start)
-
-    def home(h, start):
+    def part_across(start):
+        send(PER_HEAD + 22, part_out, part_in, part_sem.at[0], across, start)
+
+    def home(slot, start):
+        head, plane = (1, y) if slot == 1 else (2 * y, y if slot == 0 else 1 - y)
         for i in range(2):
             for f in range(2):
                 send(
-                    PER_HEAD * h + 23 + 2 * i + f,
-                    result.at[h, i],
-                    merged.at[h, model, :, lanes(2 * half + x % 2)],
-                    o_sem.at[h, model, half],
-                    (f, x % 2, y, z, 2 * core + i),
+                    PER_HEAD * slot + 23 + 2 * i + f,
+                    result.at[slot, i],
+                    merged.at[head, model, :, lanes(2 * half + x % 2)],
+                    o_sem.at[head, model, half],
+                    (f, x % 2, plane, z, 2 * core + i),
                     start,
                     True,
                 )
@@ -223,9 +230,10 @@
         for i in (near, 1 - near):
             arrive(kv.at[h, :, 0, 0, i], x_sem.at[h, i])
             ring_out(h, i, True)
-        for i in (near, 1 - near):
-            arrive(queries.at[h, 0, i], q_sem.at[h, 0, i])
-            query_across(h, i, True)
+
+    def queries_in(group, side):
+        for i in range(2):
+            arrive(queries.at[group, side, i], q_sem.at[group, side, i])
 
     def neighbours_in(h):
         for i in (near, 1 - near):
@@ -244,59 +252,65 @@
         for i in range(2):
             arrive(kv.at[h, :, block, 1, i], relay_sem.at[h, block, i])
 
-    def update(h, low, count):
+    def update(h, low, count, sides=(0, 1)):
+        group = h % 2
         keys = kv[h, 0, low : low + count].reshape(count * 4 * ROWS, HD)
         values = kv[h, 1, low : low + count].reshape(count * 4 * ROWS, HD)
         values = jnp.concatenate([values, jnp.ones_like(values)], axis=1)
-        for side in range(2):
+        for side in sides:
             for i in range(2):
                 scores = lax.dot_general(
-                    queries[h, side, i], keys, NT, preferred_element_type=jnp.float32
+                    queries[group, side, i], keys, NT, preferred_element_type=jnp.float32
                 )
-                old = best[side, i][:, :1]
+                old = best[group, side, i][:, :1]
                 new = jnp.maximum(old, jnp.max(scores, axis=1, keepdims=True))
                 weights = jnp.exp2(scores * SCALE - new * SCALE).astype(jnp.bfloat16)
                 keep = jnp.exp2((old - new) * SCALE)
-                best[side, i] = jnp.broadcast_to(new, best.shape[2:])
-                accum[side, i] = accum[side, i] * keep + jnp.dot(
+                best[group, side, i] = jnp.broadcast_to(new, best.shape[3:])
+                accum[group, side, i] = accum[group, side, i] * keep + jnp.dot(
                     weights, values, preferred_element_type=jnp.float32
                 )
 
     lane = lax.broadcasted_iota(jnp.int32, (ROWS, HD), 1)
 
     def outcome(side, i):
-        total = accum[side, i][:, HD:]
-        return accum[side, i][:, :HD] / total, best[side, i] * SCALE + jnp.log2(total)
-
-    def part(h):
+        total = accum[1, side, i][:, HD:]
+        return accum[1, side, i][:, :HD] / total, best[1, side, i] * SCALE + jnp.log2(total)
+
+    def part():
         packed = jnp.zeros((ROWS, HD), jnp.float32)
         for i in range(2):
             value, rest = outcome(1, i)
-            part_out[h, i] = value.astype(jnp.bfloat16)
+            part_out[i] = value.astype(jnp.bfloat16)
             for j in range(3):
                 piece = rest.astype(jnp.bfloat16).astype(jnp.float32)
                 packed = jnp.where(lane == 3 * i + j, piece, packed)
                 rest = rest - piece
-        part_out[h, 2] = packed.astype(jnp.bfloat16)
-        part_across(h, True)
-        for i in range(2):
-            own_value[i], own_sum[i] = outcome(0, i)
-
-    def combine(h):
-        arrive(part_in.at[h], part_sem.at[h])
-        packed = part_in[h, 2].astype(jnp.float32)
-        for i in range(2):
+        part_out[2] = packed.astype(jnp.bfloat16)
+        part_across(True)
+
+    def combine():
+        arrive(part_in, part_sem.at[0])
+        packed = part_in[2].astype(jnp.float32)
+        for i in range(2):
+            value, log_sum = outcome(0, i)
             other = (
                 packed[:, 3 * i : 3 * i + 1]
                 + packed[:, 3 * i + 1 : 3 * i + 2]
                 + packed[:, 3 * i + 2 : 3 * i + 3]
             )
-            top = jnp.maximum(own_sum[i], other)
-            mine = jnp.exp2(own_sum[i] - top)
+            top = jnp.maximum(log_sum, other)
+            mine = jnp.exp2(log_sum - top)
             theirs = jnp.exp2(other - top)
-            mixed = own_value[i] * mine + part_in[h, i].astype(jnp.float32) * theirs
-            result[h, i] = (mixed / (mine + theirs)).astype(jnp.bfloat16)
-        home(h, True)
+            mixed = value * mine + part_in[i].astype(jnp.float32) * theirs
+            result[1, i] = (mixed / (mine + theirs)).astype(jnp.bfloat16)
+        home(1, True)
+
+    def whole(slot):
+        for i in range(2):
+            done = accum[0, slot // 2, i]
+            result[slot, i] = (done[:, :HD] / done[:, HD:]).astype(jnp.bfloat16)
+        home(slot, True)
 
     def results_in(h):
         for m in range(2):
@@ -311,67 +325,83 @@
         for m, weight in ((0, w_control), (1, w_base)):
             rows = weight[:, h * HD : (h + 1) * HD].reshape(4 * HD, WIDTH)
             term = jnp.dot(merged[h, m], rows, preferred_element_type=jnp.float32)
-            proj[m] = term if h == 0 else proj[m] + term
-
-    for h in range(3):
-        pairs_out(h, True)
-        queries_out(h, True)
+            proj[m] = term if h == 1 else proj[m] + term
+
+    pairs_out(0, True)
+    queries_out(0, True)
+    queries_out(2, True)
+    pairs_out(1, True)
+    queries_out(1, True)
+    pairs_out(2, True)
     weights_beside(True)
     for copy in locals_in:
         copy.start()
+    best[...] = jnp.full(best.shape, NEG, jnp.float32)
+    accum[...] = jnp.zeros(accum.shape, jnp.float32)
     blocks_in(0)
 
-    def head_step(h, carry):
-        best[...] = jnp.full(best.shape, NEG, jnp.float32)
-        accum[...] = jnp.zeros(accum.shape, jnp.float32)
+    def slot_step(h, carry):
         relayed(h, 0)
-        for i in range(2):
-            arrive(queries.at[h, 1, i], q_sem.at[h, 1, i])
-        update(h, 0, 1)
-
-        @pl.when(h < 2)
-        def _():
-            blocks_in(h + 1)
-
-        neighbours_in(h)
 
         @pl.when(h == 0)
         def _():
+            queries_in(0, 0)
+
+        queries_in(h, 1)
+        update(h, 0, 1)
+
+        @pl.when(h == 0)
+        def _():
+            blocks_in(1)
+            neighbours_in(0)
+            queries_in(1, 0)
+            for i in range(2):
+                query_across(i, True)
             weights_across(True)
-
-        @pl.when(h == 1)
-        def _():
-            for c in range(2):
-                arrive(w_base.at[2 * (1 - half) + c, share], w_sem.at[1 + c])
-            weights_along(True)
-
-        @pl.when(h > 0)
-        def _():
-            combine(h - 1)
 
         relayed(h, 1)
         relayed(h, 2)
         update(h, 1, 2)
+
+        @pl.when(h == 0)
+        def _():
+            blocks_in(2)
+
         far_in(h)
+        neighbours_in(h + 1)
         relayed(h, 3)
         update(h, 3, 1)
-        part(h)
         return carry
 
-    lax.fori_loop(0, 3, head_step, 0)
-
-    results_in(0)
+    lax.fori_loop(0, 2, slot_step, 0)
+    part()
+    for c in range(2):
+        arrive(w_base.at[2 * (1 - half) + c, share], w_sem.at[1 + c])
+    weights_along(True)
+    relayed(2, 0)
+    update(2, 0, 1)
+    far_in(2)
+    relayed(2, 1)
+    update(2, 1, 1)
+    combine()
+    relayed(2, 2)
+    relayed(2, 3)
+    update(2, 2, 2, (1,))
+    whole(2)
+    update(2, 2, 2, (0,))
+    whole(0)
+
+    results_in(1)
     for copy in locals_in:
         copy.wait()
     arrive(w_base.at[2 * half + 1 - core], w_sem.at[0])
     for d in range(1, 4):
         rows = pl.ds(pl.multiple_of(SHARE * ((x + 4 - d) % 4), SHARE), SHARE)
         arrive(w_base.at[pl.ds(2 * (1 - half), 2), rows], w_sem.at[2 + d])
+    project(1)
+    results_in(0)
+    results_in(2)
     project(0)
-    results_in(1)
-    combine(2)
-    project(1)
-    results_in(2)
     project(2)
 
     for k in range(WIDTH // HD):
@@ -383,23 +413,26 @@
         second = x_base[:, part_lanes].astype(jnp.float32) + base_gate[row, :] * proj[1, :, part_lanes]
         base_out[:, part_lanes] = (second + first.astype(jnp.float32)).astype(jnp.bfloat16)
 
-    def finish(h, carry):
+    for h in range(3):
         pairs_out(h, False)
         queries_out(h, False)
+        home(h, False)
+
+    def finish(h, carry):
         for i in range(2):
             ring_out(h, i, False)
-            query_across(h, i, False)
             keys_on(h, i, False)
             values_on(h, i, False)
             far_on(h, i, False)
-        part_across(h, False)
-        home(h, False)
         for m in range(2):
             for f in range(2):
                 hand_over(h, m, f, False)
         return carry
 
     lax.fori_loop(0, 3, finish, 0)
+    for i in range(2):
+        query_across(i, False)
+    part_across(False)
     weights_beside(False)
     weights_across(False)
     weights_along(False)
@@ -421,13 +454,11 @@
         out_specs=(vmem, vmem),
         scratch_shapes=[
             pltpu.VMEM((3, 2, 4, 2, 2, ROWS, HD), half16),
-            pltpu.VMEM((3, 2, 2, ROWS, HD), half16),
-            pltpu.VMEM((2, 2, ROWS, HD), full32),
-            pltpu.VMEM((2, 2, ROWS, 2 * HD), full32),
-            pltpu.VMEM((2, ROWS, HD), full32),
-            pltpu.VMEM((2, ROWS, HD), full32),
-            pltpu.VMEM((3, 3, ROWS, HD), half16),
-            pltpu.VMEM((3, 3, ROWS, HD), half16),
+            pltpu.VMEM((2, 2, 2, ROWS, HD), half16),
+            pltpu.VMEM((2, 2, 2, ROWS, HD), full32),
+            pltpu.VMEM((2, 2, 2, ROWS, 2 * HD), full32),
+            pltpu.VMEM((3, ROWS, HD), half16),
+            pltpu.VMEM((3, ROWS, HD), half16),
             pltpu.VMEM((3, 2, ROWS, HD), half16),
             pltpu.VMEM((3, 2, ROWS, 4 * HD), half16),
             pltpu.VMEM((4, GROUP, WIDTH), half16),
@@ -436,11 +467,11 @@
             pltpu.VMEM((ROWS, WIDTH), half16),
             pltpu.VMEM((ROWS, WIDTH), half16),
             dma((3, 2)),
-            dma((3, 2, 2)),
+            dma((2, 2, 2)),
             dma((3, 2, 2)),
             dma((3, 2, 2)),
             dma((3, 4, 2)),
-            dma((3,)),
+            dma((1,)),
             dma((3, 2, 2)),
             dma((3, 2, 2)),
             dma((6,)),

time: 101 us -> 89 us (0.88)
  Pallas kernels: 96.3 us -> 84.4 us
    pallas_call x1, Pallas kernels: 96.3 us -> 84.4 us  [on_device(): pl.pallas_call(sublayer_kernel, out_shape=(shape, shape), in_specs=[anywh...]
where the time goes in v4:
time: 89 us; the launch traced here: 88.7 us
  Pallas kernels  84.4 us (95%)
  local copies, waits for them, and re-layouts  3.68 us (4%)
    pallas_call x1, Pallas kernels, on_device(): pl.pallas_call(sublayer_kernel, out_shape=(shape, shape), in_specs=[anywh...  84.4 us
    unnamed x2, local copies, waits for them, and re-layouts  3.68 us

profile of v4, /device:TPU:1, one launch (start us, length us, event | category | flops | bytes accessed | tf_op | source)
XLA Modules:
  0.0 88.7 jit_solution(3857790852060116095)
XLA Ops:
  0.6 84.4 %sublayer.1 = (bf16[320,768]{1,0:T(8,128)(2,1)}, bf16[320,768]{1,0:T(8,128)(2,1)}) custom-call(bf16[320,3072]{1,0:T(8,128)(2,1)} %control_x.1, bf16[3,320,1536]{2,1,0:T(8,128)(2,1)} %bitcast.6, bf16[4,384,3072]{2,1,0:T(8,128)(2,1)} %bitcast.5, f32[24,128]{1,0:T(8,128)} %bitcast.8, bf16[320,768]{1,0:T(8,128)(2,1)} %base_x.1, bf16[3,320,384]{2,1,0:T(8,128)(2,1)} %bitcast.7, ...), custom_call_target="tpu_custom_call" | custom-call | tf_op jit(solution)/shard_map/sublayer/pallas_call | solution.py:450
  85.1 1.8 %copy.12 = bf16[320,768]{1,0:T(8,128)(2,1)} copy(bf16[320,768]{1,0:T(8,128)(2,1)} %get-tuple-element.4) | data formatting | bytes 983040
  86.9 1.8 %copy.13 = bf16[320,768]{1,0:T(8,128)(2,1)} copy(bf16[320,768]{1,0:T(8,128)(2,1)} %get-tuple-element.5) | data formatting | bytes 983040

commit v5 on v4

--- a/solution.py
+++ b/solution.py
@@ -27,8 +27,7 @@
     base,
     base_w,
     base_gate,
-    control_out,
-    base_out,
+    outs,
     kv,
     queries,
     best,
@@ -57,11 +56,12 @@
     grp = lax.axis_index("grp")
     seq = lax.axis_index("seq")
     half, core, y, z, x = grp // 2, grp % 2, seq // 16, (seq // 4) % 4, seq % 4
-    model = x // 2
     here = (half, core, y, z, x)
     sibling = (half, 1 - core, y, z, x)
     above = (half, core, y, (z + 1) % 4, x)
     below = (half, core, y, (z + 3) % 4, x)
+    right = (half, core, y, z, (x + 1) % 4)
+    left = (half, core, y, z, (x + 3) % 4)
     across = (half, core, 1 - y, z, x)
 
     def ident(device):
@@ -69,11 +69,12 @@
 
     barrier = pltpu.get_barrier_semaphore()
     greeted = (
-        [sibling, above, below, across]
+        [sibling, above, below, right, left, across, (half, core, y, z, (x + 2) % 4)]
         + [(half, x % 2, p, z, 2 * core + i) for i in range(2) for p in (y, 1 - y)]
+        + [(half, z % 2, y, 2 * core + i, x) for i in range(2)]
         + [(f, x // 2, p, z, 2 * m + core) for f in range(2) for m in range(2) for p in (y, 1 - y)]
+        + [(f, z // 2, y, 2 * m + core, x) for f in range(2) for m in range(2)]
         + [(1 - half, i, y, z, x) for i in range(2)]
-        + [(half, core, y, z, (x + d) % 4) for d in range(1, 4)]
     )
     for device in greeted:
         pl.semaphore_signal(barrier, inc=1, device_id=ident(device))
@@ -112,43 +113,49 @@
     def lanes(index):
         return pl.ds(pl.multiple_of(index * HD, HD), HD)
 
-    def route(slot):
+    def route(slot, m):
         if slot == 1:
-            return 1, y
+            return 1, z % 2, (half, z // 2, y, 2 * m + core, x)
         plane = y if slot == 0 else 1 - y
-        return 2 * plane, plane
+        return 2 * plane, x % 2, (half, x // 2, plane, z, 2 * m + core)
 
     def pairs_out(slot, start):
-        head, plane = route(slot)
-        for m, ref, index in ((0, control, 3 * grp + head), (1, base, head)):
+        for m, ref, first in ((0, control, 3 * grp), (1, base, 0)):
+            head, i, device = route(slot, m)
             send(
                 PER_HEAD * slot + m,
-                ref.at[pl.ds(1, 2), :, lanes(index)],
-                kv.at[slot, :, 0, 0, x % 2],
-                x_sem.at[slot, x % 2],
-                (half, x // 2, plane, z, 2 * m + core),
+                ref.at[pl.ds(1, 2), :, lanes(first + head)],
+                kv.at[slot, :, 0, 0, i],
+                x_sem.at[slot, i],
+                device,
                 start,
                 True,
             )
 
     def queries_out(slot, start):
-        head, plane = route(slot)
-        for m, ref, index in ((0, control, 3 * grp + head), (1, base, head)):
+        for m, ref, first in ((0, control, 3 * grp), (1, base, 0)):
+            head, i, device = route(slot, m)
             send(
                 PER_HEAD * slot + 2 + m,
-                ref.at[0, :, lanes(index)],
-                queries.at[slot % 2, slot // 2, x % 2],
-                q_sem.at[slot % 2, slot // 2, x % 2],
-                (half, x // 2, plane, z, 2 * m + core),
+                ref.at[0, :, lanes(first + head)],
+                queries.at[slot % 2, slot // 2, i],
+                q_sem.at[slot % 2, slot // 2, i],
+                device,
                 start,
                 True,
             )
+
+    def ahead(h):
+        return right if h == 1 else above
+
+    def behind(h):
+        return left if h == 1 else below
 
     def ring_out(h, i, start):
         block = kv.at[h, :, 0, 0, i]
         number = PER_HEAD * h + i
-        send(number + 4, block, kv.at[h, :, 1, 0, i], z_sem.at[h, 0, i], above, start)
-        send(number + 6, block, kv.at[h, :, 2, 0, i], z_sem.at[h, 1, i], below, start)
+        send(number + 4, block, kv.at[h, :, 1, 0, i], z_sem.at[h, 0, i], ahead(h), start)
+        send(number + 6, block, kv.at[h, :, 2, 0, i], z_sem.at[h, 1, i], behind(h), start)
         send(number + 8, block, kv.at[h, :, 0, 1, i], relay_sem.at[h, 0, i], sibling, start)
 
     def query_across(i, start):
@@ -163,13 +170,13 @@
 
     def keys_on(h, i, start):
         number = PER_HEAD * h + i
-        send(number + 12, kv.at[h, 0, 1, 0, i], kv.at[h, 0, 3, 0, i], far_sem.at[h, 0, i], above, start)
+        send(number + 12, kv.at[h, 0, 1, 0, i], kv.at[h, 0, 3, 0, i], far_sem.at[h, 0, i], ahead(h), start)
         block = kv.at[h, :, 1, 0, i]
         send(number + 16, block, kv.at[h, :, 1, 1, i], relay_sem.at[h, 1, i], sibling, start)
 
     def values_on(h, i, start):
         number = PER_HEAD * h + i
-        send(number + 14, kv.at[h, 1, 2, 0, i], kv.at[h, 1, 3, 0, i], far_sem.at[h, 1, i], below, start)
+        send(number + 14, kv.at[h, 1, 2, 0, i], kv.at[h, 1, 3, 0, i], far_sem.at[h, 1, i], behind(h), start)
         block = kv.at[h, :, 2, 0, i]
         send(number + 18, block, kv.at[h, :, 2, 1, i], relay_sem.at[h, 2, i], sibling, start)
 
@@ -181,15 +188,19 @@
         send(PER_HEAD + 22, part_out, part_in, part_sem.at[0], across, start)
 
     def home(slot, start):
-        head, plane = (1, y) if slot == 1 else (2 * y, y if slot == 0 else 1 - y)
+        head, place = (1, z) if slot == 1 else (2 * y, x)
         for i in range(2):
             for f in range(2):
+                if slot == 1:
+                    owner = (f, z % 2, y, 2 * core + i, x)
+                else:
+                    owner = (f, x % 2, y if slot == 0 else 1 - y, z, 2 * core + i)
                 send(
                     PER_HEAD * slot + 23 + 2 * i + f,
                     result.at[slot, i],
-                    merged.at[head, model, :, lanes(2 * half + x % 2)],
-                    o_sem.at[head, model, half],
-                    (f, x % 2, plane, z, 2 * core + i),
+                    merged.at[head, place // 2, :, lanes(2 * half + place % 2)],
+                    o_sem.at[head, place // 2, half],
+                    owner,
                     start,
                     True,
                 )
@@ -224,10 +235,13 @@
                 last + 2 + d, block, block, w_sem.at[2 + d], (half, core, y, z, (x + d) % 4), start
             )
 
-    near = jnp.where(x // 2 == core, x % 2, 1 - x % 2)
+    def order(h):
+        place = z if h == 1 else x
+        near = jnp.where(place // 2 == core, place % 2, 1 - place % 2)
+        return near, 1 - near
 
     def blocks_in(h):
-        for i in (near, 1 - near):
+        for i in order(h):
             arrive(kv.at[h, :, 0, 0, i], x_sem.at[h, i])
             ring_out(h, i, True)
 
@@ -236,14 +250,14 @@
             arrive(queries.at[group, side, i], q_sem.at[group, side, i])
 
     def neighbours_in(h):
-        for i in (near, 1 - near):
+        for i in order(h):
             arrive(kv.at[h, :, 1, 0, i], z_sem.at[h, 0, i])
             keys_on(h, i, True)
             arrive(kv.at[h, :, 2, 0, i], z_sem.at[h, 1, i])
             values_on(h, i, True)
 
     def far_in(h):
-        for i in (near, 1 - near):
+        for i in order(h):
             for j in range(2):
                 arrive(kv.at[h, j, 3, 0, i], far_sem.at[h, j, i])
             far_on(h, i, True)
@@ -252,24 +266,28 @@
         for i in range(2):
             arrive(kv.at[h, :, block, 1, i], relay_sem.at[h, block, i])
 
-    def update(h, low, count, sides=(0, 1)):
+    def update(h, low, count, side=None):
         group = h % 2
         keys = kv[h, 0, low : low + count].reshape(count * 4 * ROWS, HD)
         values = kv[h, 1, low : low + count].reshape(count * 4 * ROWS, HD)
         values = jnp.concatenate([values, jnp.ones_like(values)], axis=1)
-        for side in sides:
-            for i in range(2):
-                scores = lax.dot_general(
-                    queries[group, side, i], keys, NT, preferred_element_type=jnp.float32
-                )
-                old = best[group, side, i][:, :1]
-                new = jnp.maximum(old, jnp.max(scores, axis=1, keepdims=True))
-                weights = jnp.exp2(scores * SCALE - new * SCALE).astype(jnp.bfloat16)
-                keep = jnp.exp2((old - new) * SCALE)
-                best[group, side, i] = jnp.broadcast_to(new, best.shape[3:])
-                accum[group, side, i] = accum[group, side, i] * keep + jnp.dot(
-                    weights, values, preferred_element_type=jnp.float32
-                )
+        if side is None:
+            tiles = [(p, i, slice(0, ROWS)) for p in range(2) for i in range(2)]
+        else:
+            cut = ROWS // 2
+            tiles = [(side, i, slice(k * cut, (k + 1) * cut)) for i in range(2) for k in range(2)]
+        for p, i, rows in tiles:
+            scores = lax.dot_general(
+                queries[group, p, i, rows], keys, NT, preferred_element_type=jnp.float32
+            )
+            old = best[group, p, i, rows][:, :1]
+            new = jnp.maximum(old, jnp.max(scores, axis=1, keepdims=True))
+            weights = jnp.exp2(scores * SCALE - new * SCALE).astype(jnp.bfloat16)
+            keep = jnp.exp2((old - new) * SCALE)
+            best[group, p, i, rows] = jnp.broadcast_to(new, (new.shape[0], HD))
+            accum[group, p, i, rows] = accum[group, p, i, rows] * keep + jnp.dot(
+                weights, values, preferred_element_type=jnp.float32
+            )
 
     lane = lax.broadcasted_iota(jnp.int32, (ROWS, HD), 1)
 
@@ -318,20 +336,21 @@
                 arrive(merged.at[h, m, :, lanes(2 * f + core)], o_sem.at[h, m, f])
                 hand_over(h, m, f, True)
 
-    def project(h):
+    def project(h, first=False):
         for m in range(2):
             for f in range(2):
                 arrive(merged.at[h, m, :, lanes(2 * f + 1 - core)], hand_sem.at[h, m, f])
         for m, weight in ((0, w_control), (1, w_base)):
-            rows = weight[:, h * HD : (h + 1) * HD].reshape(4 * HD, WIDTH)
+            rows = weight[:, lanes(h)].reshape(4 * HD, WIDTH)
             term = jnp.dot(merged[h, m], rows, preferred_element_type=jnp.float32)
-            proj[m] = term if h == 1 else proj[m] + term
+            proj[m] = term if first else proj[m] + term
 
     pairs_out(0, True)
+    pairs_out(1, True)
     queries_out(0, True)
     queries_out(2, True)
-    pairs_out(1, True)
     queries_out(1, True)
+    weights_across(True)
     pairs_out(2, True)
     weights_beside(True)
     for copy in locals_in:
@@ -339,103 +358,88 @@
     best[...] = jnp.full(best.shape, NEG, jnp.float32)
     accum[...] = jnp.zeros(accum.shape, jnp.float32)
     blocks_in(0)
-
-    def slot_step(h, carry):
-        relayed(h, 0)
-
-        @pl.when(h == 0)
-        def _():
-            queries_in(0, 0)
-
-        queries_in(h, 1)
-        update(h, 0, 1)
-
-        @pl.when(h == 0)
-        def _():
-            blocks_in(1)
-            neighbours_in(0)
-            queries_in(1, 0)
-            for i in range(2):
-                query_across(i, True)
-            weights_across(True)
-
-        relayed(h, 1)
-        relayed(h, 2)
-        update(h, 1, 2)
-
-        @pl.when(h == 0)
-        def _():
-            blocks_in(2)
-
-        far_in(h)
-        neighbours_in(h + 1)
-        relayed(h, 3)
-        update(h, 3, 1)
-        return carry
-
-    lax.fori_loop(0, 2, slot_step, 0)
-    part()
+    blocks_in(1)
+    queries_in(1, 0)
+    for i in range(2):
+        query_across(i, True)
+    relayed(0, 0)
+    queries_in(0, 0)
+    queries_in(0, 1)
+    update(0, 0, 1)
+    blocks_in(2)
+    neighbours_in(0)
+    neighbours_in(1)
+    relayed(0, 1)
+    relayed(0, 2)
+    update(0, 1, 2)
+    far_in(0)
+    far_in(1)
     for c in range(2):
         arrive(w_base.at[2 * (1 - half) + c, share], w_sem.at[1 + c])
     weights_along(True)
-    relayed(2, 0)
-    update(2, 0, 1)
+    relayed(0, 3)
+    update(0, 3, 1)
+    neighbours_in(2)
+    queries_in(1, 1)
+    relayed(1, 0)
+    relayed(1, 1)
+    update(1, 0, 2)
     far_in(2)
-    relayed(2, 1)
-    update(2, 1, 1)
+    relayed(1, 2)
+    relayed(1, 3)
+    update(1, 2, 2)
+    part()
+    for block in range(4):
+        relayed(2, block)
+    update(2, 0, 2, 1)
+    update(2, 2, 2, 1)
+    whole(2)
     combine()
-    relayed(2, 2)
-    relayed(2, 3)
-    update(2, 2, 2, (1,))
-    whole(2)
-    update(2, 2, 2, (0,))
+    update(2, 0, 2, 0)
+    update(2, 2, 2, 0)
     whole(0)
 
-    results_in(1)
+    for h in range(3):
+        pairs_out(h, False)
+        queries_out(h, False)
+        for i in range(2):
+            ring_out(h, i, False)
+            keys_on(h, i, False)
+            values_on(h, i, False)
+            far_on(h, i, False)
+    for i in range(2):
+        query_across(i, False)
+    part_across(False)
+    weights_beside(False)
+    weights_across(False)
+    weights_along(False)
     for copy in locals_in:
         copy.wait()
     arrive(w_base.at[2 * half + 1 - core], w_sem.at[0])
     for d in range(1, 4):
         rows = pl.ds(pl.multiple_of(SHARE * ((x + 4 - d) % 4), SHARE), SHARE)
         arrive(w_base.at[pl.ds(2 * (1 - half), 2), rows], w_sem.at[2 + d])
-    project(1)
-    results_in(0)
-    results_in(2)
-    project(0)
-    project(2)
+    results_in(1)
+    project(1, True)
+    results_in(2 * (1 - y))
+    project(2 * (1 - y))
+    results_in(2 * y)
+    project(2 * y)
 
     for k in range(WIDTH // HD):
         part_lanes = slice(k * HD, (k + 1) * HD)
         row = pl.ds(grp * (WIDTH // HD) + k, 1)
         first = x_control[:, part_lanes].astype(jnp.float32) + control_gate[row, :] * proj[0, :, part_lanes]
         first = first.astype(jnp.bfloat16)
-        control_out[:, part_lanes] = first
+        outs[0, :, part_lanes] = first
         second = x_base[:, part_lanes].astype(jnp.float32) + base_gate[row, :] * proj[1, :, part_lanes]
-        base_out[:, part_lanes] = (second + first.astype(jnp.float32)).astype(jnp.bfloat16)
+        outs[1, :, part_lanes] = (second + first.astype(jnp.float32)).astype(jnp.bfloat16)
 
     for h in range(3):
-        pairs_out(h, False)
-        queries_out(h, False)
         home(h, False)
-
-    def finish(h, carry):
-        for i in range(2):
-            ring_out(h, i, False)
-            keys_on(h, i, False)
-            values_on(h, i, False)
-            far_on(h, i, False)
         for m in range(2):
             for f in range(2):
                 hand_over(h, m, f, False)
-        return carry
-
-    lax.fori_loop(0, 3, finish, 0)
-    for i in range(2):
-        query_across(i, False)
-    part_across(False)
-    weights_beside(False)
-    weights_across(False)
-    weights_along(False)
 
 
 def on_device(
@@ -446,12 +450,11 @@
     dma = pltpu.SemaphoreType.DMA
     half16 = jnp.bfloat16
     full32 = jnp.float32
-    shape = jax.ShapeDtypeStruct((ROWS, WIDTH), half16)
-    return pl.pallas_call(
+    outs = pl.pallas_call(
         sublayer_kernel,
-        out_shape=(shape, shape),
+        out_shape=jax.ShapeDtypeStruct((2, ROWS, WIDTH), half16),
         in_specs=[anywhere, anywhere, anywhere, vmem, anywhere, anywhere, anywhere, vmem],
-        out_specs=(vmem, vmem),
+        out_specs=vmem,
         scratch_shapes=[
             pltpu.VMEM((3, 2, 4, 2, 2, ROWS, HD), half16),
             pltpu.VMEM((2, 2, 2, ROWS, HD), half16),
@@ -492,6 +495,7 @@
         base_out_w,
         base_gate.reshape(4 * WIDTH // HD, HD),
     )
+    return outs[0], outs[1]
 
 
 def solution(mesh):

time: 89 us -> 82.5 us (0.927)
  the two profiles are of different devices: /device:TPU:1 before, /device:TPU:33 now
where the time goes in v5:
time: 82.5 us; the launch traced here: 82.3 us
  Pallas kernels  79.4 us (96%)
  local copies, waits for them, and re-layouts  2.18 us (3%)
    pallas_call x1, Pallas kernels, on_device(): pl.pallas_call(sublayer_kernel, out_shape=jax.ShapeDtypeStruct((2, ROWS,...  79.4 us
    squeeze x1, local copies, waits for them, and re-layouts, on_device(): return (outs[0], outs[1])  2.18 us

profile of v5, /device:TPU:33, one launch (start us, length us, event | category | flops | bytes accessed | tf_op | source)
XLA Modules:
  0.0 82.3 jit_solution(7887483656903561331)
XLA Ops:
  0.6 79.4 %sublayer.1 = bf16[2,320,768]{2,1,0:T(8,128)(2,1)} custom-call(bf16[320,3072]{1,0:T(8,128)(2,1)} %control_x.1, bf16[3,320,1536]{2,1,0:T(8,128)(2,1)} %bitcast.10, bf16[4,384,3072]{2,1,0:T(8,128)(2,1)} %bitcast.9, f32[24,128]{1,0:T(8,128)} %bitcast.12, bf16[320,768]{1,0:T(8,128)(2,1)} %base_x.1, bf16[3,320,384]{2,1,0:T(8,128)(2,1)} %bitcast.11, ...), custom_call_target="tpu_custom_call" | custom-call | tf_op jit(solution)/shard_map/sublayer/pallas_call | solution.py:453
  80.1 2.2 %slice_bitcast_fusion = (bf16[320,768]{1,0:T(8,128)(2,1)}, bf16[320,768]{1,0:T(8,128)(2,1)}) fusion(bf16[2,320,768]{2,1,0:T(8,128)(2,1)} %sublayer.1), kind=kLoop, calls=%fused_computation | loop fusion | bytes 1966080 | tf_op jit(solution)/shard_map/squeeze | solution.py:498

commit v6 on v5

--- a/solution.py
+++ b/solution.py
@@ -336,14 +336,21 @@
                 arrive(merged.at[h, m, :, lanes(2 * f + core)], o_sem.at[h, m, f])
                 hand_over(h, m, f, True)
 
-    def project(h, first=False):
+    def handed(h):
         for m in range(2):
             for f in range(2):
                 arrive(merged.at[h, m, :, lanes(2 * f + 1 - core)], hand_sem.at[h, m, f])
-        for m, weight in ((0, w_control), (1, w_base)):
-            rows = weight[:, lanes(h)].reshape(4 * HD, WIDTH)
-            term = jnp.dot(merged[h, m], rows, preferred_element_type=jnp.float32)
-            proj[m] = term if first else proj[m] + term
+
+    def term(h, m, columns):
+        weight = (w_control, w_base)[m]
+        rows = weight[:, lanes(h), columns].reshape(4 * HD, -1)
+        return jnp.dot(merged[h, m], rows, preferred_element_type=jnp.float32)
+
+    def project(h, first=False):
+        handed(h)
+        for m in range(2):
+            new = term(h, m, slice(None))
+            proj[m] = new if first else proj[m] + new
 
     pairs_out(0, True)
     pairs_out(1, True)
@@ -367,12 +374,18 @@
     queries_in(0, 1)
     update(0, 0, 1)
     blocks_in(2)
+    relayed(1, 0)
+    queries_in(1, 1)
+    update(1, 0, 1)
     neighbours_in(0)
+    relayed(0, 1)
+    update(0, 1, 1)
     neighbours_in(1)
-    relayed(0, 1)
     relayed(0, 2)
-    update(0, 1, 2)
+    update(0, 2, 1)
     far_in(0)
+    relayed(1, 1)
+    update(1, 1, 1)
     far_in(1)
     for c in range(2):
         arrive(w_base.at[2 * (1 - half) + c, share], w_sem.at[1 + c])
@@ -380,22 +393,20 @@
     relayed(0, 3)
     update(0, 3, 1)
     neighbours_in(2)
-    queries_in(1, 1)
-    relayed(1, 0)
-    relayed(1, 1)
-    update(1, 0, 2)
+    relayed(1, 2)
+    update(1, 2, 1)
+    relayed(1, 3)
+    update(1, 3, 1)
+    part()
     far_in(2)
-    relayed(1, 2)
-    relayed(1, 3)
-    update(1, 2, 2)
-    part()
-    for block in range(4):
-        relayed(2, block)
-    update(2, 0, 2, 1)
+    relayed(2, 0)
+    relayed(2, 1)
+    update(2, 0, 2)
+    combine()
+    relayed(2, 2)
+    relayed(2, 3)
     update(2, 2, 2, 1)
     whole(2)
-    combine()
-    update(2, 0, 2, 0)
     update(2, 2, 2, 0)
     whole(0)
 
@@ -424,16 +435,19 @@
     results_in(2 * (1 - y))
     project(2 * (1 - y))
     results_in(2 * y)
-    project(2 * y)
-
-    for k in range(WIDTH // HD):
-        part_lanes = slice(k * HD, (k + 1) * HD)
-        row = pl.ds(grp * (WIDTH // HD) + k, 1)
-        first = x_control[:, part_lanes].astype(jnp.float32) + control_gate[row, :] * proj[0, :, part_lanes]
-        first = first.astype(jnp.bfloat16)
-        outs[0, :, part_lanes] = first
-        second = x_base[:, part_lanes].astype(jnp.float32) + base_gate[row, :] * proj[1, :, part_lanes]
-        outs[1, :, part_lanes] = (second + first.astype(jnp.float32)).astype(jnp.bfloat16)
+    handed(2 * y)
+    per_row = WIDTH // HD
+    for k in range(3):
+        columns = slice(2 * k * HD, (2 * k + 2) * HD)
+        gates = [
+            jnp.concatenate([gate[pl.ds(grp * per_row + 2 * k + j, 1), :] for j in range(2)], axis=1)
+            for gate in (control_gate, base_gate)
+        ]
+        sums = [proj[m, :, columns] + term(2 * y, m, columns) for m in range(2)]
+        first = (x_control[:, columns].astype(jnp.float32) + gates[0] * sums[0]).astype(jnp.bfloat16)
+        outs[0, :, columns] = first
+        second = x_base[:, columns].astype(jnp.float32) + gates[1] * sums[1]
+        outs[1, :, columns] = (second + first.astype(jnp.float32)).astype(jnp.bfloat16)
 
     for h in range(3):
         home(h, False)

time: 82.5 us -> 81.4 us (0.987)
  the two profiles are of different devices: /device:TPU:33 before, /device:TPU:1 now
where the time goes in v6:
time: 81.4 us; the launch traced here: 81.1 us
  Pallas kernels  78.3 us (96%)
  local copies, waits for them, and re-layouts  2.18 us (3%)
    pallas_call x1, Pallas kernels, on_device(): pl.pallas_call(sublayer_kernel, out_shape=jax.ShapeDtypeStruct((2, ROWS,...  78.3 us
    squeeze x1, local copies, waits for them, and re-layouts, on_device(): return (outs[0], outs[1])  2.18 us

profile of v6, /device:TPU:1, one launch (start us, length us, event | category | flops | bytes accessed | tf_op | source)
XLA Modules:
  0.0 81.1 jit_solution(17139640909621362680)
XLA Ops:
  0.6 78.3 %sublayer.1 = bf16[2,320,768]{2,1,0:T(8,128)(2,1)} custom-call(bf16[320,3072]{1,0:T(8,128)(2,1)} %control_x.1, bf16[3,320,1536]{2,1,0:T(8,128)(2,1)} %bitcast.10, bf16[4,384,3072]{2,1,0:T(8,128)(2,1)} %bitcast.9, f32[24,128]{1,0:T(8,128)} %bitcast.12, bf16[320,768]{1,0:T(8,128)(2,1)} %base_x.1, bf16[3,320,384]{2,1,0:T(8,128)(2,1)} %bitcast.11, ...), custom_call_target="tpu_custom_call" | custom-call | tf_op jit(solution)/shard_map/sublayer/pallas_call | solution.py:467
  79.0 2.2 %slice_bitcast_fusion = (bf16[320,768]{1,0:T(8,128)(2,1)}, bf16[320,768]{1,0:T(8,128)(2,1)}) fusion(bf16[2,320,768]{2,1,0:T(8,128)(2,1)} %sublayer.1), kind=kLoop, calls=%fused_computation | loop fusion | bytes 1966080 | tf_op jit(solution)/shard_map/squeeze | solution.py:512

commit v7 on v6

--- a/solution.py
+++ b/solution.py
@@ -374,31 +374,29 @@
     queries_in(0, 1)
     update(0, 0, 1)
     blocks_in(2)
+    neighbours_in(0)
     relayed(1, 0)
     queries_in(1, 1)
     update(1, 0, 1)
-    neighbours_in(0)
+    neighbours_in(1)
     relayed(0, 1)
-    update(0, 1, 1)
-    neighbours_in(1)
     relayed(0, 2)
-    update(0, 2, 1)
+    update(0, 1, 2)
+    neighbours_in(2)
     far_in(0)
-    relayed(1, 1)
-    update(1, 1, 1)
     far_in(1)
     for c in range(2):
         arrive(w_base.at[2 * (1 - half) + c, share], w_sem.at[1 + c])
     weights_along(True)
     relayed(0, 3)
     update(0, 3, 1)
-    neighbours_in(2)
+    relayed(1, 1)
     relayed(1, 2)
-    update(1, 2, 1)
+    update(1, 1, 2)
+    far_in(2)
     relayed(1, 3)
     update(1, 3, 1)
     part()
-    far_in(2)
     relayed(2, 0)
     relayed(2, 1)
     update(2, 0, 2)

time: 81.4 us -> 80.1 us (0.984)
  Pallas kernels: 78.3 us -> 77.1 us
    pallas_call x1, Pallas kernels: 78.3 us -> 77.1 us  [on_device(): pl.pallas_call(sublayer_kernel, out_shape=jax.ShapeDtypeStruct((2, ROWS,...]
where the time goes in v7:
time: 80.1 us; the launch traced here: 79.9 us
  Pallas kernels  77.1 us (96%)
  local copies, waits for them, and re-layouts  2.18 us (3%)
    pallas_call x1, Pallas kernels, on_device(): pl.pallas_call(sublayer_kernel, out_shape=jax.ShapeDtypeStruct((2, ROWS,...  77.1 us
    squeeze x1, local copies, waits for them, and re-layouts, on_device(): return (outs[0], outs[1])  2.18 us

profile of v7, /device:TPU:1, one launch (start us, length us, event | category | flops | bytes accessed | tf_op | source)
XLA Modules:
  0.0 79.9 jit_solution(11873775234075015017)
XLA Ops:
  0.6 77.1 %sublayer.1 = bf16[2,320,768]{2,1,0:T(8,128)(2,1)} custom-call(bf16[320,3072]{1,0:T(8,128)(2,1)} %control_x.1, bf16[3,320,1536]{2,1,0:T(8,128)(2,1)} %bitcast.10, bf16[4,384,3072]{2,1,0:T(8,128)(2,1)} %bitcast.9, f32[24,128]{1,0:T(8,128)} %bitcast.12, bf16[320,768]{1,0:T(8,128)(2,1)} %base_x.1, bf16[3,320,384]{2,1,0:T(8,128)(2,1)} %bitcast.11, ...), custom_call_target="tpu_custom_call" | custom-call | tf_op jit(solution)/shard_map/sublayer/pallas_call | solution.py:465
  77.7 2.2 %slice_bitcast_fusion = (bf16[320,768]{1,0:T(8,128)(2,1)}, bf16[320,768]{1,0:T(8,128)(2,1)}) fusion(bf16[2,320,768]{2,1,0:T(8,128)(2,1)} %sublayer.1), kind=kLoop, calls=%fused_computation | loop fusion | bytes 1966080 | tf_op jit(solution)/shard_map/squeeze | solution.py:510

commit v8 on v7

--- a/solution.py
+++ b/solution.py
@@ -266,28 +266,24 @@
         for i in range(2):
             arrive(kv.at[h, :, block, 1, i], relay_sem.at[h, block, i])
 
-    def update(h, low, count, side=None):
+    def update(h, block):
         group = h % 2
-        keys = kv[h, 0, low : low + count].reshape(count * 4 * ROWS, HD)
-        values = kv[h, 1, low : low + count].reshape(count * 4 * ROWS, HD)
+        keys = kv[h, 0, block].reshape(4 * ROWS, HD)
+        values = kv[h, 1, block].reshape(4 * ROWS, HD)
         values = jnp.concatenate([values, jnp.ones_like(values)], axis=1)
-        if side is None:
-            tiles = [(p, i, slice(0, ROWS)) for p in range(2) for i in range(2)]
-        else:
-            cut = ROWS // 2
-            tiles = [(side, i, slice(k * cut, (k + 1) * cut)) for i in range(2) for k in range(2)]
-        for p, i, rows in tiles:
-            scores = lax.dot_general(
-                queries[group, p, i, rows], keys, NT, preferred_element_type=jnp.float32
-            )
-            old = best[group, p, i, rows][:, :1]
-            new = jnp.maximum(old, jnp.max(scores, axis=1, keepdims=True))
-            weights = jnp.exp2(scores * SCALE - new * SCALE).astype(jnp.bfloat16)
-            keep = jnp.exp2((old - new) * SCALE)
-            best[group, p, i, rows] = jnp.broadcast_to(new, (new.shape[0], HD))
-            accum[group, p, i, rows] = accum[group, p, i, rows] * keep + jnp.dot(
-                weights, values, preferred_element_type=jnp.float32
-            )
+        for p in range(2):
+            for i in range(2):
+                scores = lax.dot_general(
+                    queries[group, p, i], keys, NT, preferred_element_type=jnp.float32
+                )
+                old = best[group, p, i][:, :1]
+                new = jnp.maximum(old, jnp.max(scores, axis=1, keepdims=True))
+                weights = jnp.exp2(scores * SCALE - new * SCALE).astype(jnp.bfloat16)
+                keep = jnp.exp2((old - new) * SCALE)
+                best[group, p, i] = jnp.broadcast_to(new, (ROWS, HD))
+                accum[group, p, i] = accum[group, p, i] * keep + jnp.dot(
+                    weights, values, preferred_element_type=jnp.float32
+                )
 
     lane = lax.broadcasted_iota(jnp.int32, (ROWS, HD), 1)
 
@@ -369,43 +365,62 @@
     queries_in(1, 0)
     for i in range(2):
         query_across(i, True)
-    relayed(0, 0)
     queries_in(0, 0)
     queries_in(0, 1)
-    update(0, 0, 1)
-    blocks_in(2)
-    neighbours_in(0)
-    relayed(1, 0)
-    queries_in(1, 1)
-    update(1, 0, 1)
-    neighbours_in(1)
-    relayed(0, 1)
-    relayed(0, 2)
-    update(0, 1, 2)
-    neighbours_in(2)
-    far_in(0)
-    far_in(1)
-    for c in range(2):
-        arrive(w_base.at[2 * (1 - half) + c, share], w_sem.at[1 + c])
-    weights_along(True)
-    relayed(0, 3)
-    update(0, 3, 1)
-    relayed(1, 1)
-    relayed(1, 2)
-    update(1, 1, 2)
-    far_in(2)
-    relayed(1, 3)
-    update(1, 3, 1)
-    part()
-    relayed(2, 0)
-    relayed(2, 1)
-    update(2, 0, 2)
-    combine()
-    relayed(2, 2)
-    relayed(2, 3)
-    update(2, 2, 2, 1)
+
+    steps = (
+        (0, 0), (1, 0), (0, 1), (0, 2), (1, 1), (0, 3), (1, 2), (1, 3), (2, 0), (2, 1), (2, 2), (2, 3)
+    )
+
+    def pick(t, which):
+        found = jnp.int32(steps[0][which])
+        for k, entry in enumerate(steps):
+            found = jnp.where(t == k, entry[which], found)
+        return found
+
+    def step(t, carry):
+        slot, block = pick(t, 0), pick(t, 1)
+
+        @pl.when(t == 1)
+        def _():
+            blocks_in(2)
+            neighbours_in(0)
+            queries_in(1, 1)
+
+        @pl.when(t == 2)
+        def _():
+            neighbours_in(1)
+
+        @pl.when(t == 4)
+        def _():
+            neighbours_in(2)
+            far_in(0)
+
+        @pl.when(t == 5)
+        def _():
+            far_in(1)
+            for c in range(2):
+                arrive(w_base.at[2 * (1 - half) + c, share], w_sem.at[1 + c])
+            weights_along(True)
+
+        @pl.when(t == 7)
+        def _():
+            far_in(2)
+
+        @pl.when(t == 8)
+        def _():
+            part()
+
+        @pl.when(t == 10)
+        def _():
+            combine()
+
+        relayed(slot, block)
+        update(slot, block)
+        return carry
+
+    lax.fori_loop(0, len(steps), step, 0)
     whole(2)
-    update(2, 2, 2, 0)
     whole(0)
 
     for h in range(3):

time: 80.1 us -> 82.1 us (1.025)
  Pallas kernels: 77.1 us -> 79 us
    pallas_call x1, Pallas kernels: 77.1 us -> 79 us  [on_device(): pl.pallas_call(sublayer_kernel, out_shape=jax.ShapeDtypeStruct((2, ROWS,...]
where the time goes in v8:
time: 82.1 us; the launch traced here: 81.8 us
  Pallas kernels  79 us (96%)
  local copies, waits for them, and re-layouts  2.18 us (3%)
    pallas_call x1, Pallas kernels, on_device(): pl.pallas_call(sublayer_kernel, out_shape=jax.ShapeDtypeStruct((2, ROWS,...  79 us
    squeeze x1, local copies, waits for them, and re-layouts, on_device(): return (outs[0], outs[1])  2.18 us

profile of v8, /device:TPU:1, one launch (start us, length us, event | category | flops | bytes accessed | tf_op | source)
XLA Modules:
  0.0 81.8 jit_solution(485495790021385818)
XLA Ops:
  0.6 79.0 %sublayer.1 = bf16[2,320,768]{2,1,0:T(8,128)(2,1)} custom-call(bf16[320,3072]{1,0:T(8,128)(2,1)} %control_x.1, bf16[3,320,1536]{2,1,0:T(8,128)(2,1)} %bitcast.10, bf16[4,384,3072]{2,1,0:T(8,128)(2,1)} %bitcast.9, f32[24,128]{1,0:T(8,128)} %bitcast.12, bf16[320,768]{1,0:T(8,128)(2,1)} %base_x.1, bf16[3,320,384]{2,1,0:T(8,128)(2,1)} %bitcast.11, ...), custom_call_target="tpu_custom_call" | custom-call | tf_op jit(solution)/shard_map/sublayer/pallas_call | solution.py:480
  79.6 2.2 %slice_bitcast_fusion = (bf16[320,768]{1,0:T(8,128)(2,1)}, bf16[320,768]{1,0:T(8,128)(2,1)}) fusion(bf16[2,320,768]{2,1,0:T(8,128)(2,1)} %sublayer.1), kind=kLoop, calls=%fused_computation | loop fusion | bytes 1966080 | tf_op jit(solution)/shard_map/squeeze | solution.py:525

commit v9 on v8

--- a/solution.py
+++ b/solution.py
@@ -266,24 +266,23 @@
         for i in range(2):
             arrive(kv.at[h, :, block, 1, i], relay_sem.at[h, block, i])
 
-    def update(h, block):
+    def update(tiles, h, low, count):
         group = h % 2
-        keys = kv[h, 0, block].reshape(4 * ROWS, HD)
-        values = kv[h, 1, block].reshape(4 * ROWS, HD)
+        keys = kv[h, 0, pl.ds(low, count)].reshape(count * 4 * ROWS, HD)
+        values = kv[h, 1, pl.ds(low, count)].reshape(count * 4 * ROWS, HD)
         values = jnp.concatenate([values, jnp.ones_like(values)], axis=1)
-        for p in range(2):
-            for i in range(2):
-                scores = lax.dot_general(
-                    queries[group, p, i], keys, NT, preferred_element_type=jnp.float32
-                )
-                old = best[group, p, i][:, :1]
-                new = jnp.maximum(old, jnp.max(scores, axis=1, keepdims=True))
-                weights = jnp.exp2(scores * SCALE - new * SCALE).astype(jnp.bfloat16)
-                keep = jnp.exp2((old - new) * SCALE)
-                best[group, p, i] = jnp.broadcast_to(new, (ROWS, HD))
-                accum[group, p, i] = accum[group, p, i] * keep + jnp.dot(
-                    weights, values, preferred_element_type=jnp.float32
-                )
+        for p, i, rows in tiles:
+            scores = lax.dot_general(
+                queries[group, p, i, rows], keys, NT, preferred_element_type=jnp.float32
+            )
+            old = best[group, p, i, rows][:, :1]
+            new = jnp.maximum(old, jnp.max(scores, axis=1, keepdims=True))
+            weights = jnp.exp2(scores * SCALE - new * SCALE).astype(jnp.bfloat16)
+            keep = jnp.exp2((old - new) * SCALE)
+            best[group, p, i, rows] = jnp.broadcast_to(new, (new.shape[0], HD))
+            accum[group, p, i, rows] = accum[group, p, i, rows] * keep + jnp.dot(
+                weights, values, preferred_element_type=jnp.float32
+            )
 
     lane = lax.broadcasted_iota(jnp.int32, (ROWS, HD), 1)
 
@@ -353,24 +352,20 @@
     queries_out(0, True)
     queries_out(2, True)
     queries_out(1, True)
-    weights_across(True)
-    pairs_out(2, True)
-    weights_beside(True)
     for copy in locals_in:
         copy.start()
     best[...] = jnp.full(best.shape, NEG, jnp.float32)
     accum[...] = jnp.zeros(accum.shape, jnp.float32)
     blocks_in(0)
     blocks_in(1)
+    pairs_out(2, True)
     queries_in(1, 0)
     for i in range(2):
         query_across(i, True)
     queries_in(0, 0)
     queries_in(0, 1)
 
-    steps = (
-        (0, 0), (1, 0), (0, 1), (0, 2), (1, 1), (0, 3), (1, 2), (1, 3), (2, 0), (2, 1), (2, 2), (2, 3)
-    )
+    steps = ((0, 0), (1, 0), (0, 1), (0, 2), (1, 1), (0, 3), (1, 2), (1, 3))
 
     def pick(t, which):
         found = jnp.int32(steps[0][which])
@@ -383,21 +378,26 @@
 
         @pl.when(t == 1)
         def _():
-            blocks_in(2)
+            weights_across(True)
+            weights_beside(True)
             neighbours_in(0)
             queries_in(1, 1)
 
         @pl.when(t == 2)
         def _():
+            blocks_in(2)
+
+        @pl.when(t == 3)
+        def _():
             neighbours_in(1)
 
         @pl.when(t == 4)
         def _():
+            far_in(0)
+
+        @pl.when(t == 5)
+        def _():
             neighbours_in(2)
-            far_in(0)
-
-        @pl.when(t == 5)
-        def _():
             far_in(1)
             for c in range(2):
                 arrive(w_base.at[2 * (1 - half) + c, share], w_sem.at[1 + c])
@@ -407,20 +407,27 @@
         def _():
             far_in(2)
 
-        @pl.when(t == 8)
-        def _():
-            part()
-
-        @pl.when(t == 10)
-        def _():
+        relayed(slot, block)
+        update([(p, i, slice(0, ROWS)) for p in range(2) for i in range(2)], slot, block, 1)
+        return carry
+
+    lax.fori_loop(0, len(steps), step, 0)
+    part()
+    for block in range(4):
+        relayed(2, block)
+
+    def last_step(t, carry):
+        @pl.when(t == 2)
+        def _():
+            whole(2)
             combine()
 
-        relayed(slot, block)
-        update(slot, block)
+        cut = ROWS // 2
+        tiles = [(1 - t // 2, i, slice(k * cut, (k + 1) * cut)) for i in range(2) for k in range(2)]
+        update(tiles, 2, 2 * (t % 2), 2)
         return carry
 
-    lax.fori_loop(0, len(steps), step, 0)
-    whole(2)
+    lax.fori_loop(0, 4, last_step, 0)
     whole(0)
 
     for h in range(3):

time: 82.1 us -> 77.1 us (0.939); the launches traced: 81.8 us -> 76 us
  Pallas kernels: 79 us -> 73.1 us
    pallas_call x1, Pallas kernels: 79 us -> 73.1 us  [on_device(): pl.pallas_call(sublayer_kernel, out_shape=jax.ShapeDtypeStruct((2, ROWS,...]
where the time goes in v9:
time: 77.1 us; the launch traced here: 76 us
  Pallas kernels  73.1 us (95%)
  local copies, waits for them, and re-layouts  2.18 us (3%)
    pallas_call x1, Pallas kernels, on_device(): pl.pallas_call(sublayer_kernel, out_shape=jax.ShapeDtypeStruct((2, ROWS,...  73.1 us
    squeeze x1, local copies, waits for them, and re-layouts, on_device(): return (outs[0], outs[1])  2.18 us

profile of v9, /device:TPU:1, one launch (start us, length us, event | category | flops | bytes accessed | tf_op | source)
XLA Modules:
  0.0 76.0 jit_solution(7777993757192033132)
XLA Ops:
  0.6 73.1 %sublayer.1 = bf16[2,320,768]{2,1,0:T(8,128)(2,1)} custom-call(bf16[320,3072]{1,0:T(8,128)(2,1)} %control_x.1, bf16[3,320,1536]{2,1,0:T(8,128)(2,1)} %bitcast.10, bf16[4,384,3072]{2,1,0:T(8,128)(2,1)} %bitcast.9, f32[24,128]{1,0:T(8,128)} %bitcast.12, bf16[320,768]{1,0:T(8,128)(2,1)} %base_x.1, bf16[3,320,384]{2,1,0:T(8,128)(2,1)} %bitcast.11, ...), custom_call_target="tpu_custom_call" | custom-call | tf_op jit(solution)/shard_map/sublayer/pallas_call | solution.py:487
  73.8 2.2 %slice_bitcast_fusion = (bf16[320,768]{1,0:T(8,128)(2,1)}, bf16[320,768]{1,0:T(8,128)(2,1)}) fusion(bf16[2,320,768]{2,1,0:T(8,128)(2,1)} %sublayer.1), kind=kLoop, calls=%fused_computation | loop fusion | bytes 1966080 | tf_op jit(solution)/shard_map/squeeze | solution.py:532

commit v10 on v9

--- a/solution.py
+++ b/solution.py
@@ -69,7 +69,8 @@
 
     barrier = pltpu.get_barrier_semaphore()
     greeted = (
-        [sibling, above, below, right, left, across, (half, core, y, z, (x + 2) % 4)]
+        [sibling, above, below, right, left, across]
+        + [(half, core, y, z, (x + 2) % 4), (half, core, y, (z + 2) % 4, x)]
         + [(half, x % 2, p, z, 2 * core + i) for i in range(2) for p in (y, 1 - y)]
         + [(half, z % 2, y, 2 * core + i, x) for i in range(2)]
         + [(f, x // 2, p, z, 2 * m + core) for f in range(2) for m in range(2) for p in (y, 1 - y)]
@@ -210,19 +211,21 @@
         send(PER_HEAD * h + 27 + 2 * m + f, block, block, hand_sem.at[h, m, f], sibling, start)
 
     last = 3 * PER_HEAD
-    share = pl.ds(pl.multiple_of(SHARE * x, SHARE), SHARE)
+    def share(place):
+        return pl.ds(pl.multiple_of(SHARE * place, SHARE), SHARE)
 
     def weights_beside(start):
         columns = pl.ds(pl.multiple_of((2 * half + 1 - core) * WIDTH, WIDTH), WIDTH)
         send(last, base_w.at[:, columns], w_base.at[grp], w_sem.at[0], sibling, start)
 
     def weights_across(start):
+        rows = share(jnp.where(core == 0, x, z))
         for c in range(2):
             columns = pl.ds(pl.multiple_of((2 * (1 - half) + c) * WIDTH, WIDTH), WIDTH)
             send(
                 last + 1 + c,
-                base_w.at[share, columns],
-                w_base.at[grp, share],
+                base_w.at[rows, columns],
+                w_base.at[grp, rows],
                 w_sem.at[1 + core],
                 (1 - half, c, y, z, x),
                 start,
@@ -230,10 +233,12 @@
 
     def weights_along(start):
         for d in range(1, 4):
-            block = w_base.at[pl.ds(2 * (1 - half), 2), share]
-            send(
-                last + 2 + d, block, block, w_sem.at[2 + d], (half, core, y, z, (x + d) % 4), start
-            )
+            block = w_base.at[2 * (1 - half), share(x)]
+            device = (half, core, y, z, (x + d) % 4)
+            send(last + 2 + d, block, block, w_sem.at[2 + d], device, start)
+            block = w_base.at[2 * (1 - half) + 1, share(z)]
+            device = (half, core, y, (z + d) % 4, x)
+            send(last + 5 + d, block, block, w_sem.at[5 + d], device, start)
 
     def order(h):
         place = z if h == 1 else x
@@ -400,7 +405,7 @@
             neighbours_in(2)
             far_in(1)
             for c in range(2):
-                arrive(w_base.at[2 * (1 - half) + c, share], w_sem.at[1 + c])
+                arrive(w_base.at[2 * (1 - half) + c, share((x, z)[c])], w_sem.at[1 + c])
             weights_along(True)
 
         @pl.when(t == 7)
@@ -448,8 +453,8 @@
         copy.wait()
     arrive(w_base.at[2 * half + 1 - core], w_sem.at[0])
     for d in range(1, 4):
-        rows = pl.ds(pl.multiple_of(SHARE * ((x + 4 - d) % 4), SHARE), SHARE)
-        arrive(w_base.at[pl.ds(2 * (1 - half), 2), rows], w_sem.at[2 + d])
+        arrive(w_base.at[2 * (1 - half), share((x + 4 - d) % 4)], w_sem.at[2 + d])
+        arrive(w_base.at[2 * (1 - half) + 1, share((z + 4 - d) % 4)], w_sem.at[5 + d])
     results_in(1)
     project(1, True)
     results_in(2 * (1 - y))
@@ -511,9 +516,9 @@
             dma((1,)),
             dma((3, 2, 2)),
             dma((3, 2, 2)),
-            dma((6,)),
+            dma((9,)),
             dma((4,)),
-            dma((3 * PER_HEAD + 6,)),
+            dma((3 * PER_HEAD + 9,)),
         ],
         compiler_params=pltpu.CompilerParams(
             collective_id=0, has_side_effects=True, vmem_limit_bytes=60 * 2**20

time: 77.1 us -> 80 us (1.038)
  the two profiles are of different devices: /device:TPU:1 before, /device:TPU:42 now
where the time goes in v10:
time: 80 us; the launch traced here: 79.8 us
  Pallas kernels  77 us (96%)
  local copies, waits for them, and re-layouts  2.18 us (3%)
    pallas_call x1, Pallas kernels, on_device(): pl.pallas_call(sublayer_kernel, out_shape=jax.ShapeDtypeStruct((2, ROWS,...  77 us
    squeeze x1, local copies, waits for them, and re-layouts, on_device(): return (outs[0], outs[1])  2.18 us

profile of v10, /device:TPU:42, one launch (start us, length us, event | category | flops | bytes accessed | tf_op | source)
XLA Modules:
  0.0 79.8 jit_solution(17138272724419538614)
XLA Ops:
  0.6 77.0 %sublayer.1 = bf16[2,320,768]{2,1,0:T(8,128)(2,1)} custom-call(bf16[320,3072]{1,0:T(8,128)(2,1)} %control_x.1, bf16[3,320,1536]{2,1,0:T(8,128)(2,1)} %bitcast.10, bf16[4,384,3072]{2,1,0:T(8,128)(2,1)} %bitcast.9, f32[24,128]{1,0:T(8,128)} %bitcast.12, bf16[320,768]{1,0:T(8,128)(2,1)} %base_x.1, bf16[3,320,384]{2,1,0:T(8,128)(2,1)} %bitcast.11, ...), custom_call_target="tpu_custom_call" | custom-call | tf_op jit(solution)/shard_map/sublayer/pallas_call | solution.py:492
  77.6 2.2 %slice_bitcast_fusion = (bf16[320,768]{1,0:T(8,128)(2,1)}, bf16[320,768]{1,0:T(8,128)(2,1)}) fusion(bf16[2,320,768]{2,1,0:T(8,128)(2,1)} %sublayer.1), kind=kLoop, calls=%fused_computation | loop fusion | bytes 1966080 | tf_op jit(solution)/shard_map/squeeze | solution.py:537
